TPU v7x, 128 devices: a whole 4x4x4 slice. The times are simulated.
128 devices in a mesh: row: 16 (over x, z), col: 8 (over y, core).
Axes of the slice: x: 4, y: 4, z: 4, core: 2. Of those that a mesh axis runs over, the one named last changes fastest.
Arguments:
- hamiltonian: float32 [18432, 18432], P('row', 'col'), may hold values from -6 to 6, as said below
- panel: float32 [18432, 128], P(('row', 'col')), may hold values from -0.03125 to 0.03125
Outputs:
- updated: float32 [18432, 18432], P('row', 'col')
Inputs may be any that keep to these rules, and one draw needn't show every extreme that they name: `hamiltonian`: H is symmetric: the entry at stored row p and stored column q equals the entry whose stored row and column stand for the two global indices swapped.
All inputs are finite; a program needn't handle non-finite values.
Results may differ from a plain program's by a relative error of at most 0.0002.
Values sent between devices are 32-bit elements; how exact they have to be, the bound alone decides.
A program may use at most 128 MiB of HBM per device.

v0:
```python
import jax
import jax.numpy as jnp
from jax import lax
from jax.sharding import PartitionSpec as P

B = 128


highest = lax.Precision.HIGHEST


def matmul(left, right):
    return jnp.dot(left, right, precision=highest, preferred_element_type=jnp.float32)


def shape_panel(panel_raw, global_rows, block_width):
    global_block = global_rows // block_width
    within = global_rows % block_width
    column_ids = jnp.arange(panel_raw.shape[1], dtype=jnp.int32)
    below = column_ids[None, :] < within[:, None]
    on_diagonal = column_ids[None, :] == within[:, None]
    unit_block = jnp.where(below, panel_raw, jnp.where(on_diagonal, 1.0, 0.0))
    kept = jnp.where((global_block == 1)[:, None], unit_block, 0.0)
    return jnp.where((global_block >= 2)[:, None], panel_raw, kept)


def alternate_blocks(even_rows, odd_rows, block_width):
    blocks = even_rows.shape[0] // block_width
    stacked = jnp.stack(
        [
            even_rows.reshape(blocks, block_width, even_rows.shape[1]),
            odd_rows.reshape(blocks, block_width, odd_rows.shape[1]),
        ],
        axis=1,
    )
    return stacked.reshape(2 * even_rows.shape[0], even_rows.shape[1])


def upper_inverse(gram_matrix):
    width = gram_matrix.shape[0]
    diagonal_half = jnp.diag(gram_matrix) * 0.5
    nilpotent = jnp.triu(gram_matrix, 1) / diagonal_half[:, None]
    identity_matrix = jnp.eye(width, dtype=gram_matrix.dtype)
    power = -nilpotent
    result = identity_matrix + power
    for level in range(width.bit_length()):
        power = matmul(power, power)
        result = matmul(result, identity_matrix + power)
    return result / diagonal_half[None, :]


def compact_factors(gram_matrix, cross_term):
    block_factor = upper_inverse(gram_matrix)
    middle = matmul(matmul(block_factor.T, cross_term), block_factor)
    return (block_factor, middle)


def body(hamiltonian, panel):
    rows_total = lax.axis_size("row")
    cols_total = lax.axis_size("col")
    my_row = lax.axis_index("row")
    my_col = lax.axis_index("col")
    local_rows = hamiltonian.shape[0]
    piece_rows = panel.shape[0]
    position = my_col * piece_rows + jnp.arange(piece_rows, dtype=jnp.int32)
    global_rows = (position // B * rows_total + my_row) * B + position % B
    piece = shape_panel(panel, global_rows, B)
    whole = lax.all_gather(piece, ("row", "col"), axis=0, tiled=True)
    v_rows = lax.dynamic_slice_in_dim(whole, my_row * local_rows, local_rows, 0)
    even_rows = lax.dynamic_slice_in_dim(whole, my_col * local_rows, local_rows, 0)
    odd_rows = lax.dynamic_slice_in_dim(whole, (my_col + cols_total) * local_rows, local_rows, 0)
    v_cols = alternate_blocks(even_rows, odd_rows, B)
    partial_rows = matmul(hamiltonian, v_cols)
    p_rows = lax.psum(partial_rows, "col")
    gram_part = lax.dot_general(
        v_rows,
        v_rows,
        (((0,), (0,)), ((), ())),
        precision=highest,
        preferred_element_type=jnp.float32,
    )
    cross_part = lax.dot_general(
        v_rows,
        p_rows,
        (((0,), (0,)), ((), ())),
        precision=highest,
        preferred_element_type=jnp.float32,
    )
    column_part = lax.dot_general(
        hamiltonian,
        v_rows,
        (((0,), (0,)), ((), ())),
        precision=highest,
        preferred_element_type=jnp.float32,
    )
    p_cols, gram_matrix, cross_term = lax.psum((column_part, gram_part, cross_part), "row")
    block_factor, middle = compact_factors(gram_matrix, cross_term)
    y_rows = matmul(p_rows, block_factor) - 0.5 * matmul(v_rows, middle)
    y_cols = matmul(p_cols, block_factor) - 0.5 * matmul(v_cols, middle)
    left_side = jnp.concatenate([v_rows, y_rows], axis=1)
    right_side = jnp.concatenate([y_cols, v_cols], axis=1)
    updated = hamiltonian - lax.dot_general(
        left_side,
        right_side,
        (((1,), (1,)), ((), ())),
        precision=highest,
        preferred_element_type=jnp.float32,
    )
    return updated


def solution(mesh):
    return jax.shard_map(
        body,
        mesh=mesh,
        in_specs=(P("row", "col"), P(("row", "col"), None)),
        out_specs=P("row", "col"),
        check_vma=False,
    )
```

profile of v0, /device:TPU:1, one launch (start us, length us, event | category | flops | bytes accessed | tf_op | source)
XLA Modules:
  0.0 281.0 jit_solution(10139572258187034107)
XLA Ops:
  6.5 0.0 all-gather.2.cloned.1.call-start
  6.6 1.6 select_select_fusion
  8.2 0.0 all-gather.2.cloned.1.call-update
  8.3 0.0 all-reduce.4.cloned.1.call-start
  8.3 76.7 %all-gather.2.cloned.1.call-done = f32[18432,128]{1,0:T(8,128)} async-done(((f32[144,128]{1,0:T(8,128)}), f32[18432,128]{1,0:T(8,128)}) %all-gather.2.cloned.1.call-update) | async-done | bytes 9437200 | tf_op jit(solution)/shard_map/all_gather | solution.py:68
  85.0 1.5 constant_dynamic-slice_fusion.2
  86.6 0.1 pad_maximum_fusion
  86.7 13.9 %convolution_bitcast_fusion.1 = f32[1152,128]{0,1:T(8,128)} fusion(f32[2304,128]{1,0:T(8,128)S(1)} %bitcast.51, f32[1152,2304]{1,0:T(8,128)} %param.2), kind=kOutput, calls=%fused_computation.7 | convolution fusion | flops 4076863488 | bytes 12386304 | tf_op jit(solution)/shard_map/dot_general | solution.py:13
  100.5 0.0 all-reduce.4.cloned.1.call-update
  100.5 0.2 all-reduce.6.cloned.1.call-start
  100.8 10.6 %convolution_bitcast_fusion = f32[2304,128]{0,1:T(8,128)} fusion(f32[1152,128]{1,0:T(8,128)S(1)} %get-tuple-element.8, f32[1152,2304]{1,0:T(8,128)} %param.2), kind=kOutput, calls=%fused_computation.4 | convolution fusion | flops 4076863488 | bytes 12386304 | tf_op jit(solution)/shard_map/dot_general | solution.py:89
  111.3 1.7 fusion.18
  113.1 43.7 %all-reduce.4.cloned.1.call-done = f32[1152,128]{0,1:T(8,128)} async-done(((f32[1152,128]{0,1:T(8,128)}), f32[1152,128]{0,1:T(8,128)}) %all-reduce.4.cloned.1.call-update) | async-done | bytes 589840 | tf_op jit(solution)/shard_map/psum | solution.py:74
  156.8 2.8 fusion.26
  159.6 0.0 all-reduce.6.cloned.1.call-update
  159.6 88.7 %all-reduce.6.cloned.1.call-done = (f32[2304,128]{0,1:T(8,128)}, f32[128,128]{1,0:T(8,128)}, f32[128,128]{1,0:T(8,128)}) async-done(((f32[2304,128]{0,1:T(8,128)}, f32[128,128]{1,0:T(8,128)}, f32[128,128]{1,0:T(8,128)}), (f32[2304,128]{0,1:T(8,128)}, f32[128,128]{1,0:T(8,128)}, f32[128,128]{1,0:T(8,128)})) %all-reduce.6.cloned.1.call-update) | async-done | bytes 1310736 | tf_op jit(solution)/shard_map/psum | solution.py:96
  248.4 1.9 gather_fusion
  250.3 1.2 fusion.17
  251.5 1.1 fusion.8
  252.6 0.2 fusion.19
  252.8 0.2 fusion.20
  253.0 0.0 copy-start.1
  253.0 0.2 fusion.9
  253.3 0.2 fusion.21
  253.5 0.2 fusion.10
  253.7 0.2 fusion.22
  253.9 0.2 fusion.11
  254.1 0.2 fusion.23
  254.3 0.2 fusion.12
  254.5 0.2 fusion.24
  254.7 0.2 fusion.13
  255.0 0.2 convolution_add_fusion
  255.2 0.2 fusion.14
  255.4 0.2 convolution_divide_fusion
  255.6 0.0 copy-done.1
  255.6 0.0 copy-start.2
  255.6 0.0 copy-start
  255.6 2.2 fusion.29
  257.9 0.0 copy-done.2
  257.9 0.3 fusion.27
  258.2 0.2 fusion.28
  258.4 0.0 copy-done
  258.4 1.1 fusion.25
  259.5 0.6 fusion.1
  260.1 1.1 fusion
  261.2 13.3 %convolution_subtract_fusion = f32[1152,2304]{1,0:T(8,128)} fusion(f32[1152,2304]{1,0:T(8,128)} %param.2, f32[2304,128]{1,0:T(8,128)S(1)} %bitcast.53, f32[2304,128]{1,0:T(8,128)S(1)} %fusion, f32[1152,128]{1,0:T(8,128)S(1)} %fusion.1, f32[1152,128]{1,0:T(8,128)S(1)} %get-tuple-element.8), kind=kOutput, calls=%fused_computation.1 | convolution fusion | flops 8157265920 | bytes 24772608 | tf_op jit(solution)/shard_map/dot_general | solution.py:102
  (4 shorter events, 0.1 us)
Async XLA Ops:
  6.5 78.5 %all-gather.2.cloned.1.call-start = ((), (), s32[]{:S(2)}) async-start(), calls=%async_computation | async-start | bytes 9510912 | tf_op jit(solution)/shard_map/all_gather | solution.py:68
  8.3 148.5 %all-reduce.4.cloned.1.call-start = ((), (), s32[]{:S(2)}) async-start(), calls=%async_computation.1 | async-start | bytes 1179648 | tf_op jit(solution)/shard_map/psum | solution.py:74
  100.5 147.8 %all-reduce.6.cloned.1.call-start = ((), (), s32[]{:S(2)}) async-start(), calls=%async_computation.2 | async-start | bytes 2621440 | tf_op jit(solution)/shard_map/psum | solution.py:96
  253.0 2.6 copy-start.1
  255.6 2.3 copy-start.2
  255.6 2.8 copy-start
Sparse Core Ops, SparseCore 0:
  10.5 74.5 all-gather.1
  100.7 56.0 all-reduce.3
  160.4 87.9 all-reduce.5
where the time goes:
time: 282 us; the launch traced here: 281 us
  waiting for transfers between devices  209 us (74%)
  matrix products  52.9 us (19%)
  between operations  13.4 us (5%)
  local copies, waits for them, and re-layouts  3.49 us (1%)
    psum x1, waiting for transfers between devices, body(): lax.psum((column_part, gram_part, cross_part), 'row')  88.7 us
    all_gather x1, waiting for transfers between devices, body(): whole = lax.all_gather(piece, ('row', 'col'), axis=0, tiled=True)  76.7 us
    psum x1, waiting for transfers between devices, body(): p_rows = lax.psum(partial_rows, 'col')  43.7 us
    dot_general x23, matrix products, matmul(): jnp.dot(left, right, precision=highest, preferred_element_type=jnp.float32)  24.5 us
    dot_general x1, matrix products, body(): lax.dot_general(left_side, right_side, (((1,), (1,)), ((), ())), precisio...  13.3 us
    dot_general x1, matrix products, body(): lax.dot_general(hamiltonian, v_rows, (((0,), (0,)), ((), ())), precision=...  10.6 us
  transfers between devices with their start and end apart: 3, of which 3 were waited for; matrix products, arithmetic and copies ran while one was open for 4% of the time, Pallas kernels for 0%

commit v1 on v0

v1 whole, which is shorter than its diff:
```python
import jax
import jax.numpy as jnp
from jax import lax
from jax.experimental import pallas as pl
from jax.experimental.pallas import tpu as pltpu
from jax.sharding import PartitionSpec as P

B = 128
R = 16
C = 8
MESH = pl.DeviceIdType.MESH
F32 = jnp.float32
BF16 = jnp.bfloat16
HIGHEST = lax.Precision.HIGHEST
NN = (((1,), (0,)), ((), ()))
NT = (((1,), (1,)), ((), ()))
TN = (((0,), (0,)), ((), ()))


def dot6(a, b, dims=NN):
    return lax.dot_general(a, b, dims, precision=HIGHEST, preferred_element_type=F32)


def dot1(a, b, dims=NN):
    return lax.dot_general(a, b, dims, preferred_element_type=F32)


def halves(v):
    hi = v.astype(BF16)
    return hi, (v - hi.astype(F32)).astype(BF16)


def mod4(v):
    return lax.rem(v + 8, 4)


def panel_kernel(
    h_ref, panel_ref, whi_ref, wlo_ref, zhi_ref, zlo_ref,
    hbuf, hhi, hlo, vw, rows, cols, acc, own, sib_in, ring_in, ring_out,
    part, ar1, ar2, ar3, arout, power, inverse,
    h_sem, ysend, yrecv, psend, precv, sib_send, sib_recv, ring_send, ring_recv, ar_send, ar_recv,
):
    row = lax.axis_index("row")
    col = lax.axis_index("col")
    x, z = row // 4, lax.rem(row, 4)
    y, core = col // 2, lax.rem(col, 2)
    other = col + 1 - 2 * core
    piece = panel_ref.shape[0]
    local_rows = hbuf.shape[0]
    blocks = local_rows // B

    def at_y(off):
        return (row, mod4(y + off) * 2 + core)

    peers = [(row, lax.rem(col + o, C)) for o in range(1, C)]
    x_peers = [(mod4(x + o) * 4 + z, col) for o in range(1, 4)]
    z_peers = [(x * 4 + mod4(z + o), col) for o in range(1, 4)]
    barrier = pltpu.get_barrier_semaphore()
    for peer in peers + x_peers + z_peers:
        pl.semaphore_signal(barrier, inc=1, device_id=peer, device_id_type=MESH)

    n_h = h_sem.shape[0]
    h_rows = local_rows // n_h
    h_copies = [
        pltpu.make_async_copy(
            h_ref.at[pl.ds(i * h_rows, h_rows)], hbuf.at[pl.ds(i * h_rows, h_rows)], h_sem.at[i]
        )
        for i in range(n_h)
    ]
    for copy in h_copies:
        copy.start()

    position = col * piece + lax.broadcasted_iota(jnp.int32, (piece, B), 0)
    column = lax.broadcasted_iota(jnp.int32, (piece, B), 1)
    global_block = (position >> 7) * R + row
    within = position & (B - 1)
    raw = panel_ref[...]
    unit = jnp.where(column < within, raw, jnp.where(column == within, 1.0, 0.0))
    kept = jnp.where(global_block == 1, unit, 0.0)
    v_piece = jnp.where(global_block >= 2, raw, kept)
    rows[0, col] = v_piece
    part[0] = dot6(v_piece, v_piece, TN)

    pl.semaphore_wait(barrier, len(peers) + len(x_peers) + len(z_peers))

    def remote(src, dst, send, recv, peer):
        return pltpu.make_async_remote_copy(
            src_ref=src, dst_ref=dst, send_sem=send, recv_sem=recv, device_id=peer, device_id_type=MESH
        )

    def reduce_step(ph, step):
        def wait_recv(buf, count):
            pltpu.make_async_copy(buf.at[ph, pl.ds(0, count)], buf.at[ph, pl.ds(0, count)], ar_recv.at[ph, step - 1]).wait()

        if step == 0:
            for peer in peers:
                remote(
                    part.at[ph, pl.ds(pl.multiple_of(peer[1] * 16, 16), 16)], ar1.at[ph, col],
                    ar_send.at[ph, 0], ar_recv.at[ph, 0], peer,
                ).start()
            ar1[ph, col] = part[ph, pl.ds(pl.multiple_of(col * 16, 16), 16)]
        elif step == 1:
            wait_recv(ar1, C - 1)
            ar2[ph, x] = sum(ar1[ph, i] for i in range(C))
            for peer in x_peers:
                remote(ar2.at[ph, x], ar2.at[ph, x], ar_send.at[ph, 1], ar_recv.at[ph, 1], peer).start()
        elif step == 2:
            wait_recv(ar2, 3)
            ar3[ph, z] = sum(ar2[ph, i] for i in range(4))
            for peer in z_peers:
                remote(ar3.at[ph, z], ar3.at[ph, z], ar_send.at[ph, 2], ar_recv.at[ph, 2], peer).start()
        elif step == 3:
            wait_recv(ar3, 3)
            mine = pl.ds(pl.multiple_of(col * 16, 16), 16)
            arout[ph, mine] = sum(ar3[ph, i] for i in range(4))
            for peer in peers:
                remote(arout.at[ph, mine], arout.at[ph, mine], ar_send.at[ph, 3], ar_recv.at[ph, 3], peer).start()
        else:
            pltpu.make_async_copy(
                arout.at[ph, pl.ds(0, 16 * (C - 1))], arout.at[ph, pl.ds(0, 16 * (C - 1))], ar_recv.at[ph, 3]
            ).wait()

    def reduce_finish(ph):
        for step, (buf, count) in enumerate([(ar1, C - 1), (ar2, 3), (ar3, 3), (ar1, C - 1)]):
            pltpu.make_async_copy(buf.at[ph, pl.ds(0, count)], buf.at[ph, pl.ds(0, count)], ar_send.at[ph, step]).wait()

    sign = 1 - 2 * core
    z0 = 2 * lax.rem(y, 2) + core
    dz = mod4((z - z0) * sign)
    dxs = [mod4(x - y // 2 - 2 * s) for s in range(2)]
    depth_z = jnp.minimum(dz, 4 - dz)
    depths = [jnp.minimum(dx, 4 - dx) + depth_z for dx in dxs]
    plane = [
        (mod4(x + 1) * 4 + z, col),
        (mod4(x - 1) * 4 + z, col),
        (x * 4 + mod4(z + sign), col),
        (x * 4 + mod4(z - sign), col),
    ]

    def natural(kk):
        off = (0, -1, 1, 2)[kk // 2]
        return mod4(y + off) * 2 + (core if kk % 2 == 0 else 1 - core)

    def children(i, s):
        turn = (i // 2) % 2
        dx = dxs[s]
        hop = (dx == 1) if turn == 0 else (dx == 3)
        if i % 2 == 0:
            lead = (dz == 0) & (dx == 0)
            line = (dz == 0) & hop
            plus = (lead | line) if turn == 0 else lead
            minus = lead if turn == 0 else (lead | line)
            return [plus, minus, dz == 0, (dz == 0) | (dz == 3)]
        lead = dx == 0
        return [
            (lead | hop) if turn == 0 else lead,
            lead if turn == 0 else (lead | hop),
            (dx == 0) & (dz == 0),
            (dx == 0) & ((dz == 0) | (dz == 3)),
        ]

    def forwards(i, s):
        turn = (i // 2) % 2
        if i % 2 == 0:
            return (dz == 0) | (dz == 3)
        return (dxs[s] == 0) | (dxs[s] == (1 if turn == 0 else 3))

    def plane_send(ph, i, s, source):
        k = natural(i)
        for d, flag in enumerate(children(i, s)):
            @pl.when(flag)
            def _():
                remote(
                    source, cols.at[ph, s, k], psend.at[ph, i % 4, s, d], precv.at[ph, s, k], plane[d]
                ).start()

    def piece_wait(ref, sem):
        pltpu.make_async_copy(ref, ref, sem).wait()

    def line_step(ph, kk):
        k = natural(kk)
        here = rows.at[ph, k]
        if kk > 0:
            piece_wait(here, yrecv.at[ph, k])

        def send(n, peer):
            remote(here, here, ysend.at[ph, n], yrecv.at[ph, k], peer).start()

        if kk == 0:
            send(4, at_y(1))
            send(5, at_y(-1))
        if kk == 2:
            @pl.when(core == 0)
            def _():
                send(6, at_y(1))
        if kk == 4:
            @pl.when(core == 1)
            def _():
                send(6, at_y(-1))
        if kk % 2 == 0:
            send(kk // 2, (row, other))
        for s in range(2):
            @pl.when((dxs[s] == 0) & (dz == 0))
            def _():
                plane_send(ph, kk, s, here)

    def plane_step(ph, i, level):
        for s in range(2):
            @pl.when(forwards(i, s) & (depths[s] == level))
            def _():
                k = natural(i)
                piece_wait(cols.at[ph, s, k], precv.at[ph, s, k])
                plane_send(ph, i, s, cols.at[ph, s, k])

    def gather(ph, extra):
        for tick in range(13):
            if tick < 8:
                line_step(ph, tick)
            for level, skew in ((1, 1), (2, 2), (3, 4)):
                if 0 <= tick - skew < 8:
                    plane_step(ph, tick - skew, level)
            extra(tick)
        for s in range(2):
            for i in range(8):
                k = natural(i)
                root = (dxs[s] == 0) & (dz == 0)
                @pl.when(jnp.logical_not(forwards(i, s)))
                def _():
                    piece_wait(cols.at[ph, s, k], precv.at[ph, s, k])
            @pl.when((dxs[s] == 0) & (dz == 0))
            def _():
                cols[ph, s] = rows[ph]

    def gather_finish(ph):
        for n in range(7):
            piece_wait(rows.at[ph, 0], ysend.at[ph, n])
        for i in range(4):
            for s in range(2):
                for d, flag in enumerate(children(i, s)):
                    @pl.when(flag)
                    def _():
                        two = cols.at[ph, s, pl.ds(0, 2)]
                        piece_wait(two, psend.at[ph, i, s, d])

    def split_h(i):
        h_copies[i].wait()
        hi, lo = halves(hbuf[pl.ds(i * h_rows, h_rows)])
        hhi[pl.ds(i * h_rows, h_rows)] = hi
        hlo[pl.ds(i * h_rows, h_rows)] = lo

    def first_extra(tick):
        if tick == 0:
            reduce_step(0, 0)
        if tick in (2, 4, 6, 8):
            reduce_step(0, tick // 2)
        if 4 <= tick < 4 + n_h:
            split_h(tick - 4)

    gather(0, first_extra)

    def block_rows(ph, s, b):
        flat = cols.at[ph, s].reshape(local_rows, B)
        return flat[pl.ds(b * B, B)]

    for b in range(blocks):
        for s in range(2):
            at = pl.ds((2 * b + s) * B, B)
            hi, lo = halves(block_rows(0, s, b))
            vw[at, :B] = hi
            vw[at, B:] = lo
            zhi_ref[at, :B] = hi
            zlo_ref[at, :B] = lo

    order = (2, 1, -1, 0)
    two_rows = 2 * piece

    def sum_pair(j):
        piece_wait(sib_in.at[j], sib_recv.at[j])
        total = own[j] + sib_in[j]
        ring_out[j] = total
        if order[j]:
            remote(ring_out.at[j], ring_in.at[j], ring_send.at[j], ring_recv.at[j], at_y(order[j])).start()

    for j, off in enumerate(order):
        start = pl.multiple_of(mod4(y + off) * two_rows, 32)
        take = pl.ds(start, two_rows)
        both = dot1(hhi[take], vw[...]) + dot1(hlo[take], vw[...])
        acc[...] = both[:, :B] + both[:, B:]
        mine = pl.ds(pl.multiple_of(core * piece, 8), piece)
        theirs = pl.ds(pl.multiple_of((1 - core) * piece, 8), piece)
        own[j] = acc[mine]
        ring_out[4 + j] = acc[theirs]
        remote(ring_out.at[4 + j], sib_in.at[j], sib_send.at[j], sib_recv.at[j], (row, other)).start()
        if j:
            sum_pair(j - 1)
    sum_pair(3)
    p_piece = ring_out[3]
    for j in range(3):
        piece_wait(ring_in.at[j], ring_recv.at[j])
        p_piece = p_piece + ring_in[j]
    rows[1, col] = p_piece

    eye_r = lax.broadcasted_iota(jnp.int32, (B, B), 0)
    eye_c = lax.broadcasted_iota(jnp.int32, (B, B), 1)
    gram = arout.at[0]

    def inverse_step(i):
        if i == 0:
            g = gram[...]
            half = jnp.sum(jnp.where(eye_r == eye_c, g, 0.0), axis=1, keepdims=True) * 0.5
            start = -(jnp.where(eye_c > eye_r, g, 0.0) / half)
            inverse[...] = start + jnp.where(eye_r == eye_c, 1.0, 0.0)
            power[...] = dot6(start, start)
        elif i < 7:
            now = power[...]
            inverse[...] = inverse[...] + dot6(inverse[...], now)
            if i < 6:
                power[...] = dot6(now, now)
        else:
            g = gram[...]
            half = jnp.sum(jnp.where(eye_r == eye_c, g, 0.0), axis=0, keepdims=True) * 0.5
            inverse[...] = inverse[...] / half

    def second_extra(tick):
        if tick == 0:
            part[1] = dot6(rows[0, col], rows[1, col], TN)
            reduce_step(1, 0)
        if tick in (2, 4, 6, 8):
            reduce_step(1, tick // 2)
        if 1 <= tick < 9:
            inverse_step(tick - 1)

    gather(1, second_extra)

    u = inverse[...]
    middle = dot6(dot6(u, arout[1], TN), u)
    middle = -0.5 * (middle + middle.T)
    v_rows = rows.at[0].reshape(local_rows, B)
    p_rows = rows.at[1].reshape(local_rows, B)
    chunk = 384
    for t in range(local_rows // chunk):
        at = pl.ds(t * chunk, chunk)
        v, p = v_rows[at], p_rows[at]
        hi, lo = halves(dot6(p, u) + dot6(v, middle))
        whi_ref[at, :B] = hi
        wlo_ref[at, :B] = lo
        hi, lo = halves(dot6(v, u, NT))
        whi_ref[at, B:] = hi
        wlo_ref[at, B:] = lo
    for b in range(blocks):
        for s in range(2):
            at = pl.ds((2 * b + s) * B, B)
            hi, lo = halves(block_rows(1, s, b))
            zhi_ref[at, B:] = hi
            zlo_ref[at, B:] = lo

    for ph in range(2):
        gather_finish(ph)
        reduce_finish(ph)
    for j in range(4):
        piece_wait(sib_in.at[j], sib_send.at[j])
    for j in range(3):
        piece_wait(ring_in.at[j], ring_send.at[j])


def update_kernel(h_ref, whi_ref, wlo_ref, zhi_ref, zlo_ref, out_ref):
    zhi = zhi_ref[...]
    change = dot1(whi_ref[...], zhi, NT) + dot1(wlo_ref[...], zhi, NT) + dot1(whi_ref[...], zlo_ref[...], NT)
    out_ref[...] = h_ref[...] - change


def body(hamiltonian, panel):
    m, n = hamiltonian.shape
    piece = panel.shape[0]
    vmem = pl.BlockSpec(memory_space=pltpu.VMEM)
    dma = pltpu.SemaphoreType.DMA
    n_h = 8
    whi, wlo, zhi, zlo = pl.pallas_call(
        panel_kernel,
        out_shape=[
            jax.ShapeDtypeStruct((m, 2 * B), BF16),
            jax.ShapeDtypeStruct((m, 2 * B), BF16),
            jax.ShapeDtypeStruct((n, 2 * B), BF16),
            jax.ShapeDtypeStruct((n, 2 * B), BF16),
        ],
        in_specs=[pl.BlockSpec(memory_space=pl.ANY), vmem],
        out_specs=[vmem] * 4,
        scratch_shapes=[
            pltpu.VMEM((m, n), F32),
            pltpu.VMEM((m, n), BF16),
            pltpu.VMEM((m, n), BF16),
            pltpu.VMEM((n, 2 * B), BF16),
            pltpu.VMEM((2, C, piece, B), F32),
            pltpu.VMEM((2, 2, C, piece, B), F32),
            pltpu.VMEM((2 * piece, B), F32),
            pltpu.VMEM((4, piece, B), F32),
            pltpu.VMEM((4, piece, B), F32),
            pltpu.VMEM((3, piece, B), F32),
            pltpu.VMEM((8, piece, B), F32),
            pltpu.VMEM((2, B, B), F32),
            pltpu.VMEM((2, C, 16, B), F32),
            pltpu.VMEM((2, 4, 16, B), F32),
            pltpu.VMEM((2, 4, 16, B), F32),
            pltpu.VMEM((2, B, B), F32),
            pltpu.VMEM((B, B), F32),
            pltpu.VMEM((B, B), F32),
            dma((n_h,)),
            dma((2, 7)),
            dma((2, C)),
            dma((2, 4, 2, 4)),
            dma((2, 2, C)),
            dma((4,)),
            dma((4,)),
            dma((3,)),
            dma((3,)),
            dma((2, 4)),
            dma((2, 4)),
        ],
        compiler_params=pltpu.CompilerParams(
            collective_id=0, has_side_effects=True, vmem_limit_bytes=50 * 2**20
        ),
        cost_estimate=pl.CostEstimate(flops=4 * m * n * B, bytes_accessed=4 * m * n, transcendentals=0),
        name="panel_products",
    )(hamiltonian, panel)
    tile = 2 * B
    whole = pl.BlockSpec((m, 2 * B), lambda t: (0, 0))
    strip = pl.BlockSpec((tile, 2 * B), lambda t: (t, 0))
    tall = pl.BlockSpec((m, tile), lambda t: (0, t))
    return pl.pallas_call(
        update_kernel,
        out_shape=jax.ShapeDtypeStruct((m, n), F32),
        grid=(n // tile,),
        in_specs=[tall, whole, whole, strip, strip],
        out_specs=tall,
        compiler_params=pltpu.CompilerParams(vmem_limit_bytes=40 * 2**20),
        cost_estimate=pl.CostEstimate(flops=12 * m * n * B, bytes_accessed=8 * m * n, transcendentals=0),
        name="rank_update",
    )(hamiltonian, whi, wlo, zhi, zlo)


def solution(mesh):
    return jax.shard_map(
        body,
        mesh=mesh,
        in_specs=(P("row", "col"), P(("row", "col"), None)),
        out_specs=P("row", "col"),
        check_vma=False,
    )
```

time: 282 us -> 92.1 us (0.33)
  the two profiles are of different devices: /device:TPU:1 before, /device:TPU:68 now
where the time goes in v1:
time: 92.1 us; the launch traced here: 91.9 us
  Pallas kernels  88.6 us (96%)
  local copies, waits for them, and re-layouts  3.32 us (4%)
    pallas_call x1, Pallas kernels, body(): pl.pallas_call(panel_kernel, out_shape=[jax.ShapeDtypeStruct((m, 2 * B),...  79.7 us
    pallas_call x1, Pallas kernels, body(): pl.pallas_call(update_kernel, out_shape=jax.ShapeDtypeStruct((m, n), F32)...  8.87 us
    unnamed x8, local copies, waits for them, and re-layouts  3.32 us

profile of v1, /device:TPU:68, one launch (start us, length us, event | category | flops | bytes accessed | tf_op | source)
XLA Modules:
  0.0 91.9 jit_solution(1610764625065358030)
XLA Ops:
  0.0 0.0 copy-start
  0.0 0.0 copy-start.3
  0.0 1.0 %copy-done.3 = f32[144,128]{1,0:T(8,128)S(1)} copy-done((f32[144,128]{1,0:T(8,128)S(1)}, f32[144,128]{1,0:T(8,128)}, u32[]{:S(2)}) %copy-start.3) | copy-done | bytes 73752
  1.0 79.7 %panel_products.1 = (bf16[1152,256]{1,0:T(8,128)(2,1)S(1)}, bf16[1152,256]{1,0:T(8,128)(2,1)S(1)}, bf16[2304,256]{1,0:T(8,128)(2,1)S(1)}, bf16[2304,256]{1,0:T(8,128)(2,1)S(1)}) custom-call(f32[1152,2304]{1,0:T(8,128)} %h_ref.3, f32[144,128]{1,0:T(8,128)S(1)} %copy-done.3), custom_call_target="tpu_custom_call" | custom-call | flops 1358954496 | bytes 10616832 | tf_op jit(solution)/shard_map/panel_products/pallas_call | solution.py:378
  80.8 0.0 copy-start.1
  80.8 1.0 %copy-done.1 = bf16[2304,256]{1,0:T(8,128)(2,1)} copy-done((bf16[2304,256]{1,0:T(8,128)(2,1)}, bf16[2304,256]{1,0:T(8,128)(2,1)S(1)}, u32[]{:S(2)}) %copy-start.1) | copy-done | bytes 1179672
  81.8 0.0 copy-done
  81.8 0.0 copy-start.2
  81.8 1.3 %copy-done.2 = bf16[2304,256]{1,0:T(8,128)(2,1)S(1)} copy-done((bf16[2304,256]{1,0:T(8,128)(2,1)S(1)}, bf16[2304,256]{1,0:T(8,128)(2,1)}, u32[]{:S(2)}) %copy-start.2) | copy-done | bytes 1179672
  83.1 8.9 %rank_update.1 = f32[1152,2304]{1,0:T(8,128)} custom-call(f32[1152,2304]{1,0:T(8,128)S(1)} %copy-done, bf16[1152,256]{1,0:T(8,128)(2,1)S(1)} %get-tuple-element.9.whi_ref, bf16[1152,256]{1,0:T(8,128)(2,1)S(1)} %get-tuple-element.10.wlo_ref, bf16[2304,256]{1,0:T(8,128)(2,1)S(1)} %copy-done.2, bf16[2304,256]{1,0:T(8,128)(2,1)S(1)} %get-tuple-element.12.zlo_ref), custom_call_target="tpu_custom_call" | custom-call | flops 4076863488 | bytes 21233664 | tf_op jit(solution)/shard_map/rank_update/pallas_call | solution.py:429
Async XLA Ops:
  0.0 81.8 %copy-start = (f32[1152,2304]{1,0:T(8,128)S(1)}, f32[1152,2304]{1,0:T(8,128)}, u32[]{:S(2)}) copy-start(f32[1152,2304]{1,0:T(8,128)} %h_ref.3) | copy-start | bytes 31850500
  0.0 1.0 %copy-start.3 = (f32[144,128]{1,0:T(8,128)S(1)}, f32[144,128]{1,0:T(8,128)}, u32[]{:S(2)}) copy-start(f32[144,128]{1,0:T(8,128)} %panel_ref.1) | copy-start | bytes 221188
  80.8 1.0 %copy-start.1 = (bf16[2304,256]{1,0:T(8,128)(2,1)}, bf16[2304,256]{1,0:T(8,128)(2,1)S(1)}, u32[]{:S(2)}) copy-start(bf16[2304,256]{1,0:T(8,128)(2,1)S(1)} %get-tuple-element.11.zhi_ref) | copy-start | bytes 3538948
  81.8 1.3 %copy-start.2 = (bf16[2304,256]{1,0:T(8,128)(2,1)S(1)}, bf16[2304,256]{1,0:T(8,128)(2,1)}, u32[]{:S(2)}) copy-start(bf16[2304,256]{1,0:T(8,128)(2,1)} %copy-done.1) | copy-start | bytes 3538948

commit v2 on v1

v2 whole, which is shorter than its diff:
```python
import jax
import jax.numpy as jnp
from jax import lax
from jax.experimental import pallas as pl
from jax.experimental.pallas import tpu as pltpu
from jax.sharding import PartitionSpec as P

B = 128
R = 16
C = 8
MESH = pl.DeviceIdType.MESH
F32 = jnp.float32
BF16 = jnp.bfloat16
HIGHEST = lax.Precision.HIGHEST
NN = (((1,), (0,)), ((), ()))
NT = (((1,), (1,)), ((), ()))
TN = (((0,), (0,)), ((), ()))


def dot6(a, b, dims=NN):
    return lax.dot_general(a, b, dims, precision=HIGHEST, preferred_element_type=F32)


def dot1(a, b, dims=NN):
    return lax.dot_general(a, b, dims, preferred_element_type=F32)


def halves(v):
    hi = v.astype(BF16)
    return hi, (v - hi.astype(F32)).astype(BF16)


def mod4(v):
    return lax.rem(v + 8, 4)


def panel_kernel(
    h_ref, panel_ref, out_ref,
    hhi, hlo, vw, whi, wlo, zhi, zlo, rows, cols, acc, own, sib_in, ring_in, ring_out,
    part, ar1, ar2, arout, power, inverse,
    h_sem, ysend, yrecv, lsend, psend, precv, sib_send, sib_recv, ring_send, ring_recv, ar_send, ar_recv,
):
    row = lax.axis_index("row")
    col = lax.axis_index("col")
    x, z = row // 4, lax.rem(row, 4)
    y, core = col // 2, lax.rem(col, 2)
    other = col + 1 - 2 * core
    piece = panel_ref.shape[0]
    local_rows = out_ref.shape[0]
    blocks = local_rows // B

    def at_y(off):
        return (row, mod4(y + off) * 2 + core)

    line_peers = [(row, lax.rem(col + o, C)) for o in range(1, C)]
    plane_peers = [(lax.rem(row + o, R), col) for o in range(1, R)]

    sign = 1 - 2 * core
    z0 = 2 * lax.rem(y, 2) + core
    x0s = [y // 2, y // 2 + 2]
    dz = mod4((z - z0) * sign)
    dxs = [mod4(x - x0) for x0 in x0s]
    roots = [(dx == 0) & (dz == 0) for dx in dxs]
    OFFS = (0, -1, 1, 2)

    def natural(kk):
        return mod4(y + OFFS[kk // 2]) * 2 + (core if kk % 2 == 0 else 1 - core)

    def place(kk, s):
        p, q = (dz, dxs[s]) if kk & 1 else (dxs[s], dz)
        p = mod4(-p) if (kk >> 1) & 1 else p
        q = mod4(-q) if (kk >> 2) & 1 else q
        return 4 * p + q

    def helper(code):
        return (code == 15) | (code == 6) | (code == 9)

    def neighbour(along_z, step):
        if along_z:
            return (x * 4 + mod4(z + step * sign), col)
        return (mod4(x + step) * 4 + z, col)

    y_to = lax.rem(row, C) // 2
    core_to = lax.rem(z, 2)
    col_to = y_to * 2 + core_to
    off_to = mod4(y - y_to)
    index_to = jnp.where(off_to == 0, 0, jnp.where(off_to == 3, 1, jnp.where(off_to == 1, 2, 3)))
    swap_to = core != core_to
    flip_p = lax.rem(index_to, 2) == 1
    flip_q = index_to >= 2
    helpers_to = []
    for p, q in ((3, 3), (1, 2), (2, 1)):
        p = jnp.where(flip_p, 4 - p, p)
        q = jnp.where(flip_q, 4 - q, q)
        dx_to = jnp.where(swap_to, q, p)
        dz_to = jnp.where(swap_to, p, q)
        helpers_to.append((mod4(x + dx_to) * 4 + mod4(z + dz_to * (1 - 2 * core_to)), col_to))

    barrier = pltpu.get_barrier_semaphore()
    for peer in line_peers + plane_peers:
        pl.semaphore_signal(barrier, inc=1, device_id=peer, device_id_type=MESH)
    for kk in range(8):
        for s in range(2):
            @pl.when(helper(place(kk, s)))
            def _():
                pl.semaphore_signal(
                    barrier, inc=1, device_id=(x0s[s] * 4 + z0, natural(kk)), device_id_type=MESH
                )

    n_h = h_sem.shape[0]
    h_rows = local_rows // n_h
    h_copies = [
        pltpu.make_async_copy(
            h_ref.at[pl.ds(i * h_rows, h_rows)], out_ref.at[pl.ds(i * h_rows, h_rows)], h_sem.at[i]
        )
        for i in range(n_h)
    ]
    for copy in h_copies:
        copy.start()

    position = col * piece + lax.broadcasted_iota(jnp.int32, (piece, B), 0)
    column = lax.broadcasted_iota(jnp.int32, (piece, B), 1)
    global_block = (position >> 7) * R + row
    within = position & (B - 1)
    raw = panel_ref[...]
    unit = jnp.where(column < within, raw, jnp.where(column == within, 1.0, 0.0))
    kept = jnp.where(global_block == 1, unit, 0.0)
    rows[0, col] = jnp.where(global_block >= 2, raw, kept)

    pl.semaphore_wait(barrier, len(line_peers) + len(plane_peers) + 3)

    def remote(src, dst, send, recv, peer):
        return pltpu.make_async_remote_copy(
            src_ref=src, dst_ref=dst, send_sem=send, recv_sem=recv, device_id=peer, device_id_type=MESH
        )

    def wait_for(ref, sem):
        pltpu.make_async_copy(ref, ref, sem).wait()

    mine16 = pl.ds(pl.multiple_of(col * 16, 16), 16)

    def reduce_step(ph, step):
        if step == 0:
            for peer in line_peers:
                remote(
                    part.at[ph, pl.ds(pl.multiple_of(peer[1] * 16, 16), 16)], ar1.at[ph, col],
                    ar_send.at[ph, 0], ar_recv.at[ph, 0], peer,
                ).start()
            ar1[ph, col] = part[ph, mine16]
        elif step == 1:
            wait_for(ar1.at[ph, pl.ds(0, C - 1)], ar_recv.at[ph, 0])
            ar2[ph, row] = sum(ar1[ph, i] for i in range(C))
            for peer in plane_peers:
                remote(ar2.at[ph, row], ar2.at[ph, row], ar_send.at[ph, 1], ar_recv.at[ph, 1], peer).start()
        elif step == 2:
            wait_for(ar2.at[ph, pl.ds(0, R - 1)], ar_recv.at[ph, 1])
            arout[ph, mine16] = sum(ar2[ph, i] for i in range(R))
            for peer in line_peers:
                remote(arout.at[ph, mine16], arout.at[ph, mine16], ar_send.at[ph, 2], ar_recv.at[ph, 2], peer).start()
        else:
            wait_for(arout.at[ph, pl.ds(0, 16 * (C - 1))], ar_recv.at[ph, 2])

    def reduce_finish(ph):
        wait_for(ar1.at[ph, pl.ds(0, C - 1)], ar_send.at[ph, 0])
        wait_for(ar2.at[ph, pl.ds(0, R - 1)], ar_send.at[ph, 1])
        wait_for(ar1.at[ph, pl.ds(0, C - 1)], ar_send.at[ph, 2])

    def line_step(ph, kk):
        k = natural(kk)
        here = rows.at[ph, k]
        if kk == 0:
            for n, off in enumerate((1, -1, 2)):
                remote(here, here, ysend.at[ph, n], yrecv.at[ph, k], at_y(off)).start()
            remote(here, here, ysend.at[ph, 3], yrecv.at[ph, k], (row, other)).start()
            for peer in helpers_to:
                remote(here, cols.at[ph, x // 2, k], lsend.at[ph], precv.at[ph, x // 2, k], peer).start()
        else:
            wait_for(here, yrecv.at[ph, k])
            if kk % 2 == 0:
                remote(here, here, ysend.at[ph, 3 + kk // 2], yrecv.at[ph, k], (row, other)).start()

    def plane_step(ph, kk):
        k = natural(kk)
        swap = kk & 1
        sp = -1 if (kk >> 1) & 1 else 1
        sq = -1 if (kk >> 2) & 1 else 1
        for s in range(2):
            code = place(kk, s)
            here = cols.at[ph, s, k]

            def send(source):
                toward = jnp.where((code == 0) | (code == 9), sp, -sp)
                for peer in (neighbour(not swap, sq), neighbour(not swap, -sq), neighbour(swap, toward)):
                    remote(source, here, psend.at[ph, s, kk], precv.at[ph, s, k], peer).start()

            @pl.when(roots[s])
            def _():
                send(rows.at[ph, k])

            @pl.when(helper(code))
            def _():
                wait_for(here, precv.at[ph, s, k])
                send(here)

    def gather(ph, extra):
        for tick, kk in enumerate((0, 1, 2, 4, 3, 5, 6, 7)):
            line_step(ph, kk)
            plane_step(ph, kk)
            extra(tick)

    def gather_wait(ph):
        for s in range(2):
            for kk in range(8):
                k = natural(kk)
                code = place(kk, s)
                @pl.when(jnp.logical_not(helper(code) | (code == 0)))
                def _():
                    wait_for(cols.at[ph, s, k], precv.at[ph, s, k])
            @pl.when(roots[s])
            def _():
                cols[ph, s] = rows[ph]

    def gather_finish(ph):
        for n in range(7):
            wait_for(rows.at[ph, 0], ysend.at[ph, n])
        three = cols.at[ph, 0, pl.ds(0, 3)]
        wait_for(three, lsend.at[ph])
        for kk in range(8):
            for s in range(2):
                code = place(kk, s)
                @pl.when(helper(code) | (code == 0))
                def _():
                    wait_for(three, psend.at[ph, s, kk])

    def split_h(i):
        h_copies[i].wait()
        hi, lo = halves(out_ref[pl.ds(i * h_rows, h_rows)])
        hhi[pl.ds(i * h_rows, h_rows)] = hi
        hlo[pl.ds(i * h_rows, h_rows)] = lo

    def first_extra(tick):
        if tick == 0:
            part[0] = dot6(rows[0, col], rows[0, col], TN)
            reduce_step(0, 0)
        if tick == 5:
            reduce_step(0, 1)
        split_h(tick)

    gather(0, first_extra)
    gather_wait(0)
    reduce_step(0, 2)

    def block_rows(ph, s, b):
        flat = cols.at[ph, s].reshape(local_rows, B)
        return flat[pl.ds(b * B, B)]

    for b in range(blocks):
        for s in range(2):
            at = pl.ds((2 * b + s) * B, B)
            hi, lo = halves(block_rows(0, s, b))
            vw[at, :B] = hi
            vw[at, B:] = lo
            zhi[at, :B] = hi
            zlo[at, :B] = lo

    order = (2, 1, -1, 0)
    two_rows = 2 * piece
    v_rows = rows.at[0].reshape(local_rows, B)
    p_rows = rows.at[1].reshape(local_rows, B)

    def sum_pair(j):
        wait_for(sib_in.at[j], sib_recv.at[j])
        ring_out[j] = own[j] + sib_in[j]
        if order[j]:
            remote(ring_out.at[j], ring_in.at[j], ring_send.at[j], ring_recv.at[j], at_y(order[j])).start()

    for j, off in enumerate(order):
        take = pl.ds(pl.multiple_of(mod4(y + off) * two_rows, 32), two_rows)
        both = dot1(hhi[take], vw[...]) + dot1(hlo[take], vw[...])
        acc[...] = both[:, :B] + both[:, B:]
        mine = pl.ds(pl.multiple_of(core * piece, 8), piece)
        theirs = pl.ds(pl.multiple_of((1 - core) * piece, 8), piece)
        own[j] = acc[mine]
        ring_out[4 + j] = acc[theirs]
        remote(ring_out.at[4 + j], sib_in.at[j], sib_send.at[j], sib_recv.at[j], (row, other)).start()
        cross = dot6(v_rows[take], acc[...], TN)
        part[1] = cross if j == 0 else part[1] + cross
        if j:
            sum_pair(j - 1)
    sum_pair(3)
    reduce_step(1, 0)
    p_piece = ring_out[3]
    for j in range(3):
        wait_for(ring_in.at[j], ring_recv.at[j])
        p_piece = p_piece + ring_in[j]
    rows[1, col] = p_piece

    eye_r = lax.broadcasted_iota(jnp.int32, (B, B), 0)
    eye_c = lax.broadcasted_iota(jnp.int32, (B, B), 1)
    gram = arout.at[0]

    def inverse_step(i):
        if i == 0:
            g = gram[...]
            half = jnp.sum(jnp.where(eye_r == eye_c, g, 0.0), axis=1, keepdims=True) * 0.5
            start = -(jnp.where(eye_c > eye_r, g, 0.0) / half)
            inverse[...] = start + jnp.where(eye_r == eye_c, 1.0, 0.0)
            power[...] = dot6(start, start)
        elif i < 7:
            now = power[...]
            inverse[...] = inverse[...] + dot6(inverse[...], now)
            if i < 6:
                power[...] = dot6(now, now)
        else:
            g = gram[...]
            half = jnp.sum(jnp.where(eye_r == eye_c, g, 0.0), axis=0, keepdims=True) * 0.5
            inverse[...] = inverse[...] / half

    def second_extra(tick):
        if tick == 0:
            reduce_step(1, 1)
            reduce_step(0, 3)
        if tick == 5:
            reduce_step(1, 2)
        inverse_step(tick)

    gather(1, second_extra)
    reduce_step(1, 3)

    u = inverse[...]
    middle = dot6(dot6(u, arout[1], TN), u)
    middle = -0.5 * (middle + middle.T)
    chunk = 384
    for t in range(local_rows // chunk):
        at = pl.ds(t * chunk, chunk)
        v, p = v_rows[at], p_rows[at]
        hi, lo = halves(dot6(p, u) + dot6(v, middle))
        whi[at, :B] = hi
        wlo[at, :B] = lo
        hi, lo = halves(dot6(v, u, NT))
        whi[at, B:] = hi
        wlo[at, B:] = lo

    gather_wait(1)
    for b in range(blocks):
        for s in range(2):
            at = pl.ds((2 * b + s) * B, B)
            hi, lo = halves(block_rows(1, s, b))
            zhi[at, B:] = hi
            zlo[at, B:] = lo

    def update(b, carry):
        at = pl.ds(pl.multiple_of(b * 2 * B, 2 * B), 2 * B)
        high = zhi[at]
        change = dot1(whi[...], high, NT) + dot1(wlo[...], high, NT) + dot1(whi[...], zlo[at], NT)
        out_ref[:, at] = out_ref[:, at] - change
        return carry

    lax.fori_loop(0, blocks, update, 0)

    for ph in range(2):
        gather_finish(ph)
        reduce_finish(ph)
    for j in range(4):
        wait_for(sib_in.at[j], sib_send.at[j])
    for j in range(3):
        wait_for(ring_in.at[j], ring_send.at[j])


def body(hamiltonian, panel):
    m, n = hamiltonian.shape
    piece = panel.shape[0]
    vmem = pl.BlockSpec(memory_space=pltpu.VMEM)
    dma = pltpu.SemaphoreType.DMA
    return pl.pallas_call(
        panel_kernel,
        out_shape=jax.ShapeDtypeStruct((m, n), F32),
        in_specs=[pl.BlockSpec(memory_space=pl.ANY), vmem],
        out_specs=vmem,
        scratch_shapes=[
            pltpu.VMEM((m, n), BF16),
            pltpu.VMEM((m, n), BF16),
            pltpu.VMEM((n, 2 * B), BF16),
            pltpu.VMEM((m, 2 * B), BF16),
            pltpu.VMEM((m, 2 * B), BF16),
            pltpu.VMEM((n, 2 * B), BF16),
            pltpu.VMEM((n, 2 * B), BF16),
            pltpu.VMEM((2, C, piece, B), F32),
            pltpu.VMEM((2, 2, C, piece, B), F32),
            pltpu.VMEM((2 * piece, B), F32),
            pltpu.VMEM((4, piece, B), F32),
            pltpu.VMEM((4, piece, B), F32),
            pltpu.VMEM((3, piece, B), F32),
            pltpu.VMEM((8, piece, B), F32),
            pltpu.VMEM((2, B, B), F32),
            pltpu.VMEM((2, C, 16, B), F32),
            pltpu.VMEM((2, R, 16, B), F32),
            pltpu.VMEM((2, B, B), F32),
            pltpu.VMEM((B, B), F32),
            pltpu.VMEM((B, B), F32),
            dma((8,)),
            dma((2, 7)),
            dma((2, C)),
            dma((2,)),
            dma((2, 2, C)),
            dma((2, 2, C)),
            dma((4,)),
            dma((4,)),
            dma((3,)),
            dma((3,)),
            dma((2, 3)),
            dma((2, 3)),
        ],
        compiler_params=pltpu.CompilerParams(
            collective_id=0, has_side_effects=True, vmem_limit_bytes=40 * 2**20
        ),
        cost_estimate=pl.CostEstimate(flops=16 * m * n * B, bytes_accessed=4 * m * n, transcendentals=0),
        name="panel_update",
    )(hamiltonian, panel)


def solution(mesh):
    return jax.shard_map(
        body,
        mesh=mesh,
        in_specs=(P("row", "col"), P(("row", "col"), None)),
        out_specs=P("row", "col"),
        check_vma=False,
    )
```

time: 92.1 us -> 73.3 us (0.80)
  the two profiles are of different devices: /device:TPU:68 before, /device:TPU:1 now
where the time goes in v2:
time: 73.3 us; the launch traced here: 73.2 us
  Pallas kernels  68.2 us (93%)
  local copies, waits for them, and re-layouts  5.02 us (7%)
    pallas_call x1, Pallas kernels, body(): pl.pallas_call(panel_kernel, out_shape=jax.ShapeDtypeStruct((m, n), F32),...  68.2 us
    unnamed x3, local copies, waits for them, and re-layouts  5.02 us

profile of v2, /device:TPU:1, one launch (start us, length us, event | category | flops | bytes accessed | tf_op | source)
XLA Modules:
  0.0 73.2 jit_solution(16797494909123626949)
XLA Ops:
  0.0 0.0 copy-start
  0.0 0.9 %copy-done = f32[144,128]{1,0:T(8,128)S(1)} copy-done((f32[144,128]{1,0:T(8,128)S(1)}, f32[144,128]{1,0:T(8,128)}, u32[]{:S(2)}) %copy-start) | copy-done | bytes 73752
  0.9 68.2 %panel_update.1 = f32[1152,2304]{1,0:T(8,128)S(1)} custom-call(f32[1152,2304]{1,0:T(8,128)} %h_ref.1, f32[144,128]{1,0:T(8,128)S(1)} %copy-done), custom_call_target="tpu_custom_call" | custom-call | flops 5435817984 | bytes 10616832 | tf_op jit(solution)/shard_map/panel_update/pallas_call | solution.py:375
  69.1 4.1 %copy.4 = f32[1152,2304]{1,0:T(8,128)} copy(f32[1152,2304]{1,0:T(8,128)S(1)} %panel_update.1) | data formatting | bytes 21233664
Async XLA Ops:
  0.0 0.9 %copy-start = (f32[144,128]{1,0:T(8,128)S(1)}, f32[144,128]{1,0:T(8,128)}, u32[]{:S(2)}) copy-start(f32[144,128]{1,0:T(8,128)} %panel_ref.1) | copy-start | bytes 221188

commit v3 on v2

--- a/solution.py
+++ b/solution.py
@@ -12,6 +12,17 @@
 F32 = jnp.float32
 BF16 = jnp.bfloat16
 HIGHEST = lax.Precision.HIGHEST
+
+PATTERNS = (
+    ((0, 14, 7, 3), ((1, 8, 12), (13, 10, 9), (6, 11, 4), (2, 5, 15))),
+    ((0, 7, 4, 14), ((3, 1, 12), (10, 6, 11), (8, 9, 5), (15, 2, 13))),
+    ((0, 2, 12, 11), ((4, 5, 3), (1, 14, 6), (9, 13, 8), (7, 15, 10))),
+    ((0, 14, 7, 3), ((1, 5, 12), (13, 10, 9), (4, 6, 11), (2, 8, 15))),
+    ((0, 3, 13, 11), ((1, 4, 12), (7, 2, 6), (14, 9, 5), (15, 8, 10))),
+    ((0, 14, 7, 3), ((8, 4, 12), (13, 10, 9), (6, 11, 5), (2, 1, 15))),
+    ((0, 3, 4, 10), ((1, 12, 13), (15, 2, 14), (7, 5, 8), (9, 11, 6))),
+    ((0, 14, 7, 3), ((1, 8, 12), (13, 10, 9), (6, 11, 4), (2, 5, 15))),
+)
 NN = (((1,), (0,)), ((), ()))
 NT = (((1,), (1,)), ((), ()))
 TN = (((0,), (0,)), ((), ()))
@@ -35,18 +46,20 @@
 
 
 def panel_kernel(
-    h_ref, panel_ref, out_ref,
-    hhi, hlo, vw, whi, wlo, zhi, zlo, rows, cols, acc, own, sib_in, ring_in, ring_out,
+    h_ref, panel_ref, h_out, whi, wlo, zhi, zlo,
+    hhi, hlo, vw, rows, cols, acc, sib_in, ring_in, ring_out, raw_panel,
     part, ar1, ar2, arout, power, inverse,
-    h_sem, ysend, yrecv, lsend, psend, precv, sib_send, sib_recv, ring_send, ring_recv, ar_send, ar_recv,
+    p_sem, h_sem, ysend, yrecv, lsend, psend, precv, sib_send, sib_recv, ring_send, ring_recv, ar_send, ar_recv,
 ):
     row = lax.axis_index("row")
     col = lax.axis_index("col")
     x, z = row // 4, lax.rem(row, 4)
     y, core = col // 2, lax.rem(col, 2)
     other = col + 1 - 2 * core
+    panel_copy = pltpu.make_async_copy(panel_ref, raw_panel, p_sem)
+    panel_copy.start()
     piece = panel_ref.shape[0]
-    local_rows = out_ref.shape[0]
+    local_rows = h_out.shape[0]
     blocks = local_rows // B
 
     def at_y(off):
@@ -55,53 +68,56 @@
     line_peers = [(row, lax.rem(col + o, C)) for o in range(1, C)]
     plane_peers = [(lax.rem(row + o, R), col) for o in range(1, R)]
 
-    sign = 1 - 2 * core
+    sz = 1 - 2 * core
+    sx = 1 - 2 * (y // 2)
     z0 = 2 * lax.rem(y, 2) + core
     x0s = [y // 2, y // 2 + 2]
-    dz = mod4((z - z0) * sign)
-    dxs = [mod4(x - x0) for x0 in x0s]
-    roots = [(dx == 0) & (dz == 0) for dx in dxs]
+    codes = [4 * mod4((x - x0) * sx) + mod4((z - z0) * sz) for x0 in x0s]
+    roots = [code == 0 for code in codes]
     OFFS = (0, -1, 1, 2)
 
     def natural(kk):
         return mod4(y + OFFS[kk // 2]) * 2 + (core if kk % 2 == 0 else 1 - core)
 
-    def place(kk, s):
-        p, q = (dz, dxs[s]) if kk & 1 else (dxs[s], dz)
-        p = mod4(-p) if (kk >> 1) & 1 else p
-        q = mod4(-q) if (kk >> 2) & 1 else q
-        return 4 * p + q
-
-    def helper(code):
-        return (code == 15) | (code == 6) | (code == 9)
-
-    def neighbour(along_z, step):
-        if along_z:
-            return (x * 4 + mod4(z + step * sign), col)
-        return (mod4(x + step) * 4 + z, col)
+    def chain(key, keys, values):
+        out = values[0]
+        for k, v in zip(keys[1:], values[1:]):
+            out = jnp.where(key == k, v, out)
+        return out
+
+    def helper(kk, s):
+        first, second, third = PATTERNS[kk][0][1:]
+        return (codes[s] == first) | (codes[s] == second) | (codes[s] == third)
+
+    def next_chips(kk, s):
+        heads, groups = PATTERNS[kk]
+        for n in range(3):
+            steps = [
+                4 * ((group[n] // 4 - head // 4) % 4) + (group[n] % 4 - head % 4) % 4
+                for head, group in zip(heads, groups)
+            ]
+            step = chain(codes[s], heads, steps)
+            yield (mod4(x + sx * (step // 4)) * 4 + mod4(z + sz * lax.rem(step, 4)), col)
 
     y_to = lax.rem(row, C) // 2
     core_to = lax.rem(z, 2)
     col_to = y_to * 2 + core_to
     off_to = mod4(y - y_to)
     index_to = jnp.where(off_to == 0, 0, jnp.where(off_to == 3, 1, jnp.where(off_to == 1, 2, 3)))
-    swap_to = core != core_to
-    flip_p = lax.rem(index_to, 2) == 1
-    flip_q = index_to >= 2
+    kk_to = 2 * index_to + jnp.where(core == core_to, 0, 1)
+    sx_to = 1 - 2 * (y_to // 2)
+    sz_to = 1 - 2 * core_to
     helpers_to = []
-    for p, q in ((3, 3), (1, 2), (2, 1)):
-        p = jnp.where(flip_p, 4 - p, p)
-        q = jnp.where(flip_q, 4 - q, q)
-        dx_to = jnp.where(swap_to, q, p)
-        dz_to = jnp.where(swap_to, p, q)
-        helpers_to.append((mod4(x + dx_to) * 4 + mod4(z + dz_to * (1 - 2 * core_to)), col_to))
+    for n in range(1, 4):
+        step = chain(kk_to, range(8), [heads[n] for heads, _ in PATTERNS])
+        helpers_to.append((mod4(x + sx_to * (step // 4)) * 4 + mod4(z + sz_to * lax.rem(step, 4)), col_to))
 
     barrier = pltpu.get_barrier_semaphore()
     for peer in line_peers + plane_peers:
         pl.semaphore_signal(barrier, inc=1, device_id=peer, device_id_type=MESH)
     for kk in range(8):
         for s in range(2):
-            @pl.when(helper(place(kk, s)))
+            @pl.when(helper(kk, s))
             def _():
                 pl.semaphore_signal(
                     barrier, inc=1, device_id=(x0s[s] * 4 + z0, natural(kk)), device_id_type=MESH
@@ -111,7 +127,7 @@
     h_rows = local_rows // n_h
     h_copies = [
         pltpu.make_async_copy(
-            h_ref.at[pl.ds(i * h_rows, h_rows)], out_ref.at[pl.ds(i * h_rows, h_rows)], h_sem.at[i]
+            h_ref.at[pl.ds(i * h_rows, h_rows)], h_out.at[pl.ds(i * h_rows, h_rows)], h_sem.at[i]
         )
         for i in range(n_h)
     ]
@@ -122,7 +138,8 @@
     column = lax.broadcasted_iota(jnp.int32, (piece, B), 1)
     global_block = (position >> 7) * R + row
     within = position & (B - 1)
-    raw = panel_ref[...]
+    panel_copy.wait()
+    raw = raw_panel[...]
     unit = jnp.where(column < within, raw, jnp.where(column == within, 1.0, 0.0))
     kept = jnp.where(global_block == 1, unit, 0.0)
     rows[0, col] = jnp.where(global_block >= 2, raw, kept)
@@ -165,55 +182,77 @@
         wait_for(ar2.at[ph, pl.ds(0, R - 1)], ar_send.at[ph, 1])
         wait_for(ar1.at[ph, pl.ds(0, C - 1)], ar_send.at[ph, 2])
 
+    am_root = col == col_to
+    other_root = other == col_to
+    OTHERS = (1, -1, 2)
+
+    def other_is_root(off):
+        return (mod4(y + off) == y_to) & (core == core_to)
+
+    def first_sends(ph):
+        here = rows.at[ph, col]
+        @pl.when(jnp.logical_not(am_root))
+        def _():
+            remote(here, here, ysend.at[ph, 0], yrecv.at[ph, col], (row, col_to)).start()
+        for peer in helpers_to:
+            remote(here, cols.at[ph, x // 2, col], lsend.at[ph], precv.at[ph, x // 2, col], peer).start()
+
+    def line_start(ph):
+        here = rows.at[ph, col]
+        for n, off in enumerate(OTHERS):
+            @pl.when(jnp.logical_not(other_is_root(off)))
+            def _():
+                remote(here, here, ysend.at[ph, 1 + n], yrecv.at[ph, col], at_y(off)).start()
+        @pl.when(jnp.logical_not(other_root))
+        def _():
+            remote(here, here, ysend.at[ph, 4], yrecv.at[ph, col], (row, other)).start()
+
     def line_step(ph, kk):
         k = natural(kk)
         here = rows.at[ph, k]
-        if kk == 0:
-            for n, off in enumerate((1, -1, 2)):
-                remote(here, here, ysend.at[ph, n], yrecv.at[ph, k], at_y(off)).start()
-            remote(here, here, ysend.at[ph, 3], yrecv.at[ph, k], (row, other)).start()
-            for peer in helpers_to:
-                remote(here, cols.at[ph, x // 2, k], lsend.at[ph], precv.at[ph, x // 2, k], peer).start()
-        else:
+        @pl.when(jnp.logical_not(am_root))
+        def _():
             wait_for(here, yrecv.at[ph, k])
-            if kk % 2 == 0:
-                remote(here, here, ysend.at[ph, 3 + kk // 2], yrecv.at[ph, k], (row, other)).start()
+        if kk % 2 == 0:
+            @pl.when(jnp.logical_not(other_root))
+            def _():
+                remote(here, here, ysend.at[ph, 4 + kk // 2], yrecv.at[ph, k], (row, other)).start()
 
     def plane_step(ph, kk):
         k = natural(kk)
-        swap = kk & 1
-        sp = -1 if (kk >> 1) & 1 else 1
-        sq = -1 if (kk >> 2) & 1 else 1
         for s in range(2):
-            code = place(kk, s)
             here = cols.at[ph, s, k]
 
             def send(source):
-                toward = jnp.where((code == 0) | (code == 9), sp, -sp)
-                for peer in (neighbour(not swap, sq), neighbour(not swap, -sq), neighbour(swap, toward)):
+                for peer in next_chips(kk, s):
                     remote(source, here, psend.at[ph, s, kk], precv.at[ph, s, k], peer).start()
 
             @pl.when(roots[s])
             def _():
+                if kk:
+                    wait_for(rows.at[ph, k], yrecv.at[ph, k])
                 send(rows.at[ph, k])
 
-            @pl.when(helper(code))
+            @pl.when(helper(kk, s))
             def _():
                 wait_for(here, precv.at[ph, s, k])
                 send(here)
 
+    ORDER = (0, 1, 2, 4, 3, 5, 6, 7)
+
     def gather(ph, extra):
-        for tick, kk in enumerate((0, 1, 2, 4, 3, 5, 6, 7)):
-            line_step(ph, kk)
+        first_sends(ph)
+        for tick, kk in enumerate(ORDER):
             plane_step(ph, kk)
+            if tick == 4:
+                line_start(ph)
             extra(tick)
 
     def gather_wait(ph):
         for s in range(2):
             for kk in range(8):
                 k = natural(kk)
-                code = place(kk, s)
-                @pl.when(jnp.logical_not(helper(code) | (code == 0)))
+                @pl.when(jnp.logical_not(helper(kk, s) | roots[s]))
                 def _():
                     wait_for(cols.at[ph, s, k], precv.at[ph, s, k])
             @pl.when(roots[s])
@@ -221,20 +260,22 @@
                 cols[ph, s] = rows[ph]
 
     def gather_finish(ph):
-        for n in range(7):
-            wait_for(rows.at[ph, 0], ysend.at[ph, n])
+        sent = [jnp.logical_not(am_root)] + [jnp.logical_not(other_is_root(off)) for off in OTHERS]
+        for n, flag in enumerate(sent + [jnp.logical_not(other_root)] * 4):
+            @pl.when(flag)
+            def _():
+                wait_for(rows.at[ph, 0], ysend.at[ph, n])
         three = cols.at[ph, 0, pl.ds(0, 3)]
         wait_for(three, lsend.at[ph])
         for kk in range(8):
             for s in range(2):
-                code = place(kk, s)
-                @pl.when(helper(code) | (code == 0))
+                @pl.when(helper(kk, s) | roots[s])
                 def _():
                     wait_for(three, psend.at[ph, s, kk])
 
     def split_h(i):
         h_copies[i].wait()
-        hi, lo = halves(out_ref[pl.ds(i * h_rows, h_rows)])
+        hi, lo = halves(h_out[pl.ds(i * h_rows, h_rows)])
         hhi[pl.ds(i * h_rows, h_rows)] = hi
         hlo[pl.ds(i * h_rows, h_rows)] = lo
 
@@ -248,7 +289,6 @@
 
     gather(0, first_extra)
     gather_wait(0)
-    reduce_step(0, 2)
 
     def block_rows(ph, s, b):
         flat = cols.at[ph, s].reshape(local_rows, B)
@@ -268,26 +308,31 @@
     v_rows = rows.at[0].reshape(local_rows, B)
     p_rows = rows.at[1].reshape(local_rows, B)
 
+    def part_of(j, which):
+        start = mod4(y + order[j]) * two_rows + which * piece
+        return pl.ds(pl.multiple_of(start, 16), piece)
+
     def sum_pair(j):
         wait_for(sib_in.at[j], sib_recv.at[j])
-        ring_out[j] = own[j] + sib_in[j]
+        ring_out[j] = acc[part_of(j, core)] + sib_in[j]
         if order[j]:
             remote(ring_out.at[j], ring_in.at[j], ring_send.at[j], ring_recv.at[j], at_y(order[j])).start()
 
     for j, off in enumerate(order):
         take = pl.ds(pl.multiple_of(mod4(y + off) * two_rows, 32), two_rows)
         both = dot1(hhi[take], vw[...]) + dot1(hlo[take], vw[...])
-        acc[...] = both[:, :B] + both[:, B:]
-        mine = pl.ds(pl.multiple_of(core * piece, 8), piece)
-        theirs = pl.ds(pl.multiple_of((1 - core) * piece, 8), piece)
-        own[j] = acc[mine]
-        ring_out[4 + j] = acc[theirs]
-        remote(ring_out.at[4 + j], sib_in.at[j], sib_send.at[j], sib_recv.at[j], (row, other)).start()
-        cross = dot6(v_rows[take], acc[...], TN)
-        part[1] = cross if j == 0 else part[1] + cross
+        acc[take] = both[:, :B] + both[:, B:]
+        remote(
+            acc.at[part_of(j, 1 - core)], sib_in.at[j], sib_send.at[j], sib_recv.at[j], (row, other)
+        ).start()
         if j:
             sum_pair(j - 1)
+        if j == 2:
+            reduce_step(0, 2)
     sum_pair(3)
+    for kk in ORDER[1:]:
+        line_step(0, kk)
+    part[1] = dot6(v_rows[...], acc[...], TN)
     reduce_step(1, 0)
     p_piece = ring_out[3]
     for j in range(3):
@@ -325,6 +370,8 @@
         inverse_step(tick)
 
     gather(1, second_extra)
+    for kk in ORDER[1:]:
+        line_step(1, kk)
     reduce_step(1, 3)
 
     u = inverse[...]
@@ -349,15 +396,6 @@
             zhi[at, B:] = hi
             zlo[at, B:] = lo
 
-    def update(b, carry):
-        at = pl.ds(pl.multiple_of(b * 2 * B, 2 * B), 2 * B)
-        high = zhi[at]
-        change = dot1(whi[...], high, NT) + dot1(wlo[...], high, NT) + dot1(whi[...], zlo[at], NT)
-        out_ref[:, at] = out_ref[:, at] - change
-        return carry
-
-    lax.fori_loop(0, blocks, update, 0)
-
     for ph in range(2):
         gather_finish(ph)
         reduce_finish(ph)
@@ -367,39 +405,71 @@
         wait_for(ring_in.at[j], ring_send.at[j])
 
 
+def update_kernel(h_ref, whi, wlo, zhi, zlo, out_ref, tiles, sem):
+    width = tiles.shape[2]
+    slots = tiles.shape[0]
+    steps = h_ref.shape[1] // width
+
+    def copy(b):
+        slot = lax.rem(b, slots)
+        return pltpu.make_async_copy(
+            tiles.at[slot], out_ref.at[:, pl.ds(pl.multiple_of(b * width, width), width)], sem.at[slot]
+        )
+
+    def step(b, carry):
+        @pl.when(b >= slots)
+        def _():
+            copy(b - slots).wait()
+
+        at = pl.ds(pl.multiple_of(b * width, width), width)
+        high = zhi[at]
+        change = dot1(whi[...], high, NT) + dot1(wlo[...], high, NT) + dot1(whi[...], zlo[at], NT)
+        tiles[lax.rem(b, slots)] = h_ref[:, at] - change
+        copy(b).start()
+        return carry
+
+    lax.fori_loop(0, steps, step, 0)
+    for b in range(steps - slots, steps):
+        copy(b).wait()
+
+
 def body(hamiltonian, panel):
     m, n = hamiltonian.shape
     piece = panel.shape[0]
     vmem = pl.BlockSpec(memory_space=pltpu.VMEM)
+    hbm = pl.BlockSpec(memory_space=pl.ANY)
     dma = pltpu.SemaphoreType.DMA
-    return pl.pallas_call(
+    operands = pl.pallas_call(
         panel_kernel,
-        out_shape=jax.ShapeDtypeStruct((m, n), F32),
-        in_specs=[pl.BlockSpec(memory_space=pl.ANY), vmem],
-        out_specs=vmem,
+        out_shape=[
+            jax.ShapeDtypeStruct((m, n), F32),
+            jax.ShapeDtypeStruct((m, 2 * B), BF16),
+            jax.ShapeDtypeStruct((m, 2 * B), BF16),
+            jax.ShapeDtypeStruct((n, 2 * B), BF16),
+            jax.ShapeDtypeStruct((n, 2 * B), BF16),
+        ],
+        in_specs=[hbm, hbm],
+        out_specs=[vmem] * 5,
         scratch_shapes=[
             pltpu.VMEM((m, n), BF16),
             pltpu.VMEM((m, n), BF16),
             pltpu.VMEM((n, 2 * B), BF16),
-            pltpu.VMEM((m, 2 * B), BF16),
-            pltpu.VMEM((m, 2 * B), BF16),
-            pltpu.VMEM((n, 2 * B), BF16),
-            pltpu.VMEM((n, 2 * B), BF16),
             pltpu.VMEM((2, C, piece, B), F32),
             pltpu.VMEM((2, 2, C, piece, B), F32),
-            pltpu.VMEM((2 * piece, B), F32),
-            pltpu.VMEM((4, piece, B), F32),
+            pltpu.VMEM((m, B), F32),
             pltpu.VMEM((4, piece, B), F32),
             pltpu.VMEM((3, piece, B), F32),
-            pltpu.VMEM((8, piece, B), F32),
+            pltpu.VMEM((4, piece, B), F32),
+            pltpu.VMEM((piece, B), F32),
             pltpu.VMEM((2, B, B), F32),
             pltpu.VMEM((2, C, 16, B), F32),
             pltpu.VMEM((2, R, 16, B), F32),
             pltpu.VMEM((2, B, B), F32),
             pltpu.VMEM((B, B), F32),
             pltpu.VMEM((B, B), F32),
+            dma,
             dma((8,)),
-            dma((2, 7)),
+            dma((2, 8)),
             dma((2, C)),
             dma((2,)),
             dma((2, 2, C)),
@@ -414,9 +484,19 @@
         compiler_params=pltpu.CompilerParams(
             collective_id=0, has_side_effects=True, vmem_limit_bytes=40 * 2**20
         ),
-        cost_estimate=pl.CostEstimate(flops=16 * m * n * B, bytes_accessed=4 * m * n, transcendentals=0),
-        name="panel_update",
+        cost_estimate=pl.CostEstimate(flops=8 * m * n * B, bytes_accessed=4 * m * n, transcendentals=0),
+        name="panel_products",
     )(hamiltonian, panel)
+    return pl.pallas_call(
+        update_kernel,
+        out_shape=jax.ShapeDtypeStruct((m, n), F32),
+        in_specs=[vmem] * 5,
+        out_specs=hbm,
+        scratch_shapes=[pltpu.VMEM((3, m, 2 * B), F32), dma((3,))],
+        compiler_params=pltpu.CompilerParams(vmem_limit_bytes=24 * 2**20),
+        cost_estimate=pl.CostEstimate(flops=12 * m * n * B, bytes_accessed=4 * m * n, transcendentals=0),
+        name="rank_update",
+    )(*operands)
 
 
 def solution(mesh):

time: 73.3 us -> 71.6 us (0.977)
  local copies, waits for them, and re-layouts: 5.02 us -> 0.88 us
  Pallas kernels: 68.2 us -> 70.4 us
    unnamed x3 -> x2, local copies, waits for them, and re-layouts: 5.02 us -> 0.88 us
    pallas_call x1 -> x2, Pallas kernels: 68.2 us -> 70.4 us  [the longest x1 63.2 us: body(): pl.pallas_call(panel_kernel, out_shape=[jax.ShapeDtypeStruct((m, n), F32)...]
where the time goes in v3:
time: 71.6 us; the launch traced here: 71.4 us
  Pallas kernels  70.4 us (98%)
  local copies, waits for them, and re-layouts  0.88 us (1%)
    pallas_call x1, Pallas kernels, body(): pl.pallas_call(panel_kernel, out_shape=[jax.ShapeDtypeStruct((m, n), F32)...  63.2 us
    pallas_call x1, Pallas kernels, body(): pl.pallas_call(update_kernel, out_shape=jax.ShapeDtypeStruct((m, n), F32)...  7.21 us

profile of v3, /device:TPU:1, one launch (start us, length us, event | category | flops | bytes accessed | tf_op | source)
XLA Modules:
  0.0 71.4 jit_solution(3557187283032754171)
XLA Ops:
  0.0 0.0 copy-start
  0.0 0.9 %copy-done = f32[144,128]{1,0:T(8,128)S(1)} copy-done((f32[144,128]{1,0:T(8,128)S(1)}, f32[144,128]{1,0:T(8,128)}, u32[]{:S(2)}) %copy-start) | copy-done | bytes 73752
  0.9 63.2 %panel_products.1 = (f32[1152,2304]{1,0:T(8,128)S(1)}, bf16[1152,256]{1,0:T(8,128)(2,1)S(1)}, bf16[1152,256]{1,0:T(8,128)(2,1)S(1)}, bf16[2304,256]{1,0:T(8,128)(2,1)S(1)}, bf16[2304,256]{1,0:T(8,128)(2,1)S(1)}) custom-call(f32[1152,2304]{1,0:T(8,128)} %h_ref.1, f32[144,128]{1,0:T(8,128)S(1)} %copy-done), custom_call_target="tpu_custom_call" | custom-call | flops 2717908992 | bytes 10616832 | tf_op jit(solution)/shard_map/panel_products/pallas_call | solution.py:442
  64.1 7.2 %rank_update.1 = f32[1152,2304]{1,0:T(8,128)} custom-call(f32[1152,2304]{1,0:T(8,128)S(1)} %get-tuple-element.10.h_ref, bf16[1152,256]{1,0:T(8,128)(2,1)S(1)} %get-tuple-element.11.whi, bf16[1152,256]{1,0:T(8,128)(2,1)S(1)} %get-tuple-element.12.wlo, bf16[2304,256]{1,0:T(8,128)(2,1)S(1)} %get-tuple-element.13.zhi, bf16[2304,256]{1,0:T(8,128)(2,1)S(1)} %get-tuple-element.14.zlo), custom_call_target="tpu_custom_call" | custom-call | flops 4076863488 | bytes 10616832 | tf_op jit(solution)/shard_map/rank_update/pallas_call | solution.py:490
Async XLA Ops:
  0.0 0.9 %copy-start = (f32[144,128]{1,0:T(8,128)S(1)}, f32[144,128]{1,0:T(8,128)}, u32[]{:S(2)}) copy-start(f32[144,128]{1,0:T(8,128)} %panel_ref.1) | copy-start | bytes 221188

commit v4 on v3

--- a/solution.py
+++ b/solution.py
@@ -14,14 +14,14 @@
 HIGHEST = lax.Precision.HIGHEST
 
 PATTERNS = (
-    ((0, 14, 7, 3), ((1, 8, 12), (13, 10, 9), (6, 11, 4), (2, 5, 15))),
-    ((0, 7, 4, 14), ((3, 1, 12), (10, 6, 11), (8, 9, 5), (15, 2, 13))),
-    ((0, 2, 12, 11), ((4, 5, 3), (1, 14, 6), (9, 13, 8), (7, 15, 10))),
-    ((0, 14, 7, 3), ((1, 5, 12), (13, 10, 9), (4, 6, 11), (2, 8, 15))),
-    ((0, 3, 13, 11), ((1, 4, 12), (7, 2, 6), (14, 9, 5), (15, 8, 10))),
-    ((0, 14, 7, 3), ((8, 4, 12), (13, 10, 9), (6, 11, 5), (2, 1, 15))),
-    ((0, 3, 4, 10), ((1, 12, 13), (15, 2, 14), (7, 5, 8), (9, 11, 6))),
-    ((0, 14, 7, 3), ((1, 8, 12), (13, 10, 9), (6, 11, 4), (2, 5, 15))),
+    ((0, 2, 4, 8, 11, 12, 13), ((), (1, 3, 6, 14), (5, 7), (), (10, 15), (), (9,))),
+    ((0, 1, 4, 7, 8, 11, 12, 15), ((), (2, 13), (5,), (3, 6), (9,), (10,), (), (14,))),
+    ((0, 2, 4, 11, 13), ((3,), (1, 6, 14), (5,), (7, 8, 10, 15), (9, 12))),
+    ((0, 5, 7, 8, 14), ((1,), (9,), (3, 4, 6, 11), (12,), (2, 10, 13, 15))),
+    ((0, 2, 4, 9, 12), ((), (1, 3, 6, 14), (5, 7, 8), (10, 11, 13), (15,))),
+    ((0, 5, 7, 8, 14), ((3,), (1, 9), (4, 6), (11, 12), (2, 10, 13, 15))),
+    ((0, 5, 7, 14), ((8, 12), (1, 6, 9, 13), (3, 4, 11), (2, 10, 15))),
+    ((0, 9, 10, 15), ((1, 4, 12), (5, 8, 13), (2, 6, 11, 14), (3, 7))),
 )
 NN = (((1,), (0,)), ((), ()))
 NT = (((1,), (1,)), ((), ()))
@@ -85,19 +85,30 @@
             out = jnp.where(key == k, v, out)
         return out
 
+    def among(key, keys):
+        found = key == keys[0]
+        for k in keys[1:]:
+            found = found | (key == k)
+        return found
+
     def helper(kk, s):
-        first, second, third = PATTERNS[kk][0][1:]
-        return (codes[s] == first) | (codes[s] == second) | (codes[s] == third)
+        return among(codes[s], PATTERNS[kk][0][1:])
 
     def next_chips(kk, s):
         heads, groups = PATTERNS[kk]
-        for n in range(3):
-            steps = [
-                4 * ((group[n] // 4 - head // 4) % 4) + (group[n] % 4 - head % 4) % 4
-                for head, group in zip(heads, groups)
-            ]
-            step = chain(codes[s], heads, steps)
-            yield (mod4(x + sx * (step // 4)) * 4 + mod4(z + sz * lax.rem(step, 4)), col)
+        for n in range(max(len(group) for group in groups)):
+            pairs = [(head, group[n]) for head, group in zip(heads, groups) if len(group) > n]
+            keys = [head for head, _ in pairs]
+            steps = [4 * ((to // 4 - head // 4) % 4) + (to % 4 - head % 4) % 4 for head, to in pairs]
+            step = chain(codes[s], keys, steps)
+            peer = (mod4(x + sx * (step // 4)) * 4 + mod4(z + sz * lax.rem(step, 4)), col)
+            yield peer, None if len(keys) == len(heads) else among(codes[s], keys)
+
+    def when(flag, act):
+        if flag is None:
+            act()
+        else:
+            pl.when(flag)(act)
 
     y_to = lax.rem(row, C) // 2
     core_to = lax.rem(z, 2)
@@ -107,10 +118,14 @@
     kk_to = 2 * index_to + jnp.where(core == core_to, 0, 1)
     sx_to = 1 - 2 * (y_to // 2)
     sz_to = 1 - 2 * core_to
+    counts = [len(heads) - 1 for heads, _ in PATTERNS]
+    count_to = chain(kk_to, range(8), counts)
     helpers_to = []
-    for n in range(1, 4):
-        step = chain(kk_to, range(8), [heads[n] for heads, _ in PATTERNS])
-        helpers_to.append((mod4(x + sx_to * (step // 4)) * 4 + mod4(z + sz_to * lax.rem(step, 4)), col_to))
+    for n in range(max(counts)):
+        having = [kk for kk in range(8) if counts[kk] > n]
+        step = chain(kk_to, having, [PATTERNS[kk][0][n + 1] for kk in having])
+        peer = (mod4(x + sx_to * (step // 4)) * 4 + mod4(z + sz_to * lax.rem(step, 4)), col_to)
+        helpers_to.append((peer, None if len(having) == 8 else count_to > n))
 
     barrier = pltpu.get_barrier_semaphore()
     for peer in line_peers + plane_peers:
@@ -144,7 +159,7 @@
     kept = jnp.where(global_block == 1, unit, 0.0)
     rows[0, col] = jnp.where(global_block >= 2, raw, kept)
 
-    pl.semaphore_wait(barrier, len(line_peers) + len(plane_peers) + 3)
+    pl.semaphore_wait(barrier, len(line_peers) + len(plane_peers) + count_to)
 
     def remote(src, dst, send, recv, peer):
         return pltpu.make_async_remote_copy(
@@ -194,8 +209,9 @@
         @pl.when(jnp.logical_not(am_root))
         def _():
             remote(here, here, ysend.at[ph, 0], yrecv.at[ph, col], (row, col_to)).start()
-        for peer in helpers_to:
-            remote(here, cols.at[ph, x // 2, col], lsend.at[ph], precv.at[ph, x // 2, col], peer).start()
+        for peer, flag in helpers_to:
+            copy = remote(here, cols.at[ph, x // 2, col], lsend.at[ph], precv.at[ph, x // 2, col], peer)
+            when(flag, copy.start)
 
     def line_start(ph):
         here = rows.at[ph, col]
@@ -224,8 +240,8 @@
             here = cols.at[ph, s, k]
 
             def send(source):
-                for peer in next_chips(kk, s):
-                    remote(source, here, psend.at[ph, s, kk], precv.at[ph, s, k], peer).start()
+                for peer, flag in next_chips(kk, s):
+                    when(flag, remote(source, here, psend.at[ph, s, kk], precv.at[ph, s, k], peer).start)
 
             @pl.when(roots[s])
             def _():
@@ -265,13 +281,19 @@
             @pl.when(flag)
             def _():
                 wait_for(rows.at[ph, 0], ysend.at[ph, n])
-        three = cols.at[ph, 0, pl.ds(0, 3)]
-        wait_for(three, lsend.at[ph])
+        for count in sorted(set(counts)):
+            @pl.when(count_to == count)
+            def _():
+                wait_for(cols.at[ph, 0, pl.ds(0, count)], lsend.at[ph])
         for kk in range(8):
+            heads, groups = PATTERNS[kk]
+            sizes = sorted(set(len(group) for group in groups) - {0})
             for s in range(2):
-                @pl.when(helper(kk, s) | roots[s])
-                def _():
-                    wait_for(three, psend.at[ph, s, kk])
+                for size in sizes:
+                    keys = [head for head, group in zip(heads, groups) if len(group) == size]
+                    @pl.when(among(codes[s], keys))
+                    def _():
+                        wait_for(cols.at[ph, 0, pl.ds(0, size)], psend.at[ph, s, kk])
 
     def split_h(i):
         h_copies[i].wait()
@@ -282,12 +304,12 @@
     def first_extra(tick):
         if tick == 0:
             part[0] = dot6(rows[0, col], rows[0, col], TN)
+        if tick == 4:
             reduce_step(0, 0)
-        if tick == 5:
-            reduce_step(0, 1)
         split_h(tick)
 
     gather(0, first_extra)
+    reduce_step(0, 1)
     gather_wait(0)
 
     def block_rows(ph, s, b):
@@ -327,13 +349,12 @@
         ).start()
         if j:
             sum_pair(j - 1)
-        if j == 2:
-            reduce_step(0, 2)
     sum_pair(3)
     for kk in ORDER[1:]:
         line_step(0, kk)
     part[1] = dot6(v_rows[...], acc[...], TN)
     reduce_step(1, 0)
+    reduce_step(0, 2)
     p_piece = ring_out[3]
     for j in range(3):
         wait_for(ring_in.at[j], ring_recv.at[j])
@@ -365,11 +386,10 @@
         if tick == 0:
             reduce_step(1, 1)
             reduce_step(0, 3)
-        if tick == 5:
-            reduce_step(1, 2)
         inverse_step(tick)
 
     gather(1, second_extra)
+    reduce_step(1, 2)
     for kk in ORDER[1:]:
         line_step(1, kk)
     reduce_step(1, 3)

time: 71.6 us -> 66.3 us (0.926)
  Pallas kernels: 70.4 us -> 65.1 us
    pallas_call x1, Pallas kernels: 63.2 us -> 57.9 us  [body(): pl.pallas_call(panel_kernel, out_shape=[jax.ShapeDtypeStruct((m, n), F32)...]
where the time goes in v4:
time: 66.3 us; the launch traced here: 66.2 us
  Pallas kernels  65.1 us (98%)
  local copies, waits for them, and re-layouts  0.88 us (1%)
    pallas_call x1, Pallas kernels, body(): pl.pallas_call(panel_kernel, out_shape=[jax.ShapeDtypeStruct((m, n), F32)...  57.9 us
    pallas_call x1, Pallas kernels, body(): pl.pallas_call(update_kernel, out_shape=jax.ShapeDtypeStruct((m, n), F32)...  7.22 us

profile of v4, /device:TPU:1, one launch (start us, length us, event | category | flops | bytes accessed | tf_op | source)
XLA Modules:
  0.0 66.2 jit_solution(8594498938389190364)
XLA Ops:
  0.0 0.0 copy-start
  0.0 0.9 %copy-done = f32[144,128]{1,0:T(8,128)S(1)} copy-done((f32[144,128]{1,0:T(8,128)S(1)}, f32[144,128]{1,0:T(8,128)}, u32[]{:S(2)}) %copy-start) | copy-done | bytes 73752
  0.9 57.9 %panel_products.1 = (f32[1152,2304]{1,0:T(8,128)S(1)}, bf16[1152,256]{1,0:T(8,128)(2,1)S(1)}, bf16[1152,256]{1,0:T(8,128)(2,1)S(1)}, bf16[2304,256]{1,0:T(8,128)(2,1)S(1)}, bf16[2304,256]{1,0:T(8,128)(2,1)S(1)}) custom-call(f32[1152,2304]{1,0:T(8,128)} %h_ref.1, f32[144,128]{1,0:T(8,128)S(1)} %copy-done), custom_call_target="tpu_custom_call" | custom-call | flops 2717908992 | bytes 10616832 | tf_op jit(solution)/shard_map/panel_products/pallas_call | solution.py:462
  58.8 7.2 %rank_update.1 = f32[1152,2304]{1,0:T(8,128)} custom-call(f32[1152,2304]{1,0:T(8,128)S(1)} %get-tuple-element.10.h_ref, bf16[1152,256]{1,0:T(8,128)(2,1)S(1)} %get-tuple-element.11.whi, bf16[1152,256]{1,0:T(8,128)(2,1)S(1)} %get-tuple-element.12.wlo, bf16[2304,256]{1,0:T(8,128)(2,1)S(1)} %get-tuple-element.13.zhi, bf16[2304,256]{1,0:T(8,128)(2,1)S(1)} %get-tuple-element.14.zlo), custom_call_target="tpu_custom_call" | custom-call | flops 4076863488 | bytes 10616832 | tf_op jit(solution)/shard_map/rank_update/pallas_call | solution.py:510
Async XLA Ops:
  0.0 0.9 %copy-start = (f32[144,128]{1,0:T(8,128)S(1)}, f32[144,128]{1,0:T(8,128)}, u32[]{:S(2)}) copy-start(f32[144,128]{1,0:T(8,128)} %panel_ref.1) | copy-start | bytes 221188

commit v5 on v4

--- a/solution.py
+++ b/solution.py
@@ -48,7 +48,7 @@
 def panel_kernel(
     h_ref, panel_ref, h_out, whi, wlo, zhi, zlo,
     hhi, hlo, vw, rows, cols, acc, sib_in, ring_in, ring_out, raw_panel,
-    part, ar1, ar2, arout, power, inverse,
+    part, ar1, ar2, ar3, arout, power, inverse,
     p_sem, h_sem, ysend, yrecv, lsend, psend, precv, sib_send, sib_recv, ring_send, ring_recv, ar_send, ar_recv,
 ):
     row = lax.axis_index("row")
@@ -66,6 +66,8 @@
         return (row, mod4(y + off) * 2 + core)
 
     line_peers = [(row, lax.rem(col + o, C)) for o in range(1, C)]
+    x_peers = [(mod4(x + o) * 4 + z, col) for o in range(1, 4)]
+    z_peers = [(x * 4 + mod4(z + o), col) for o in range(1, 4)]
     plane_peers = [(lax.rem(row + o, R), col) for o in range(1, R)]
 
     sz = 1 - 2 * core
@@ -181,21 +183,25 @@
             ar1[ph, col] = part[ph, mine16]
         elif step == 1:
             wait_for(ar1.at[ph, pl.ds(0, C - 1)], ar_recv.at[ph, 0])
-            ar2[ph, row] = sum(ar1[ph, i] for i in range(C))
-            for peer in plane_peers:
-                remote(ar2.at[ph, row], ar2.at[ph, row], ar_send.at[ph, 1], ar_recv.at[ph, 1], peer).start()
+            ar2[ph, x] = sum(ar1[ph, i] for i in range(C))
+            for peer in x_peers:
+                remote(ar2.at[ph, x], ar2.at[ph, x], ar_send.at[ph, 1], ar_recv.at[ph, 1], peer).start()
         elif step == 2:
-            wait_for(ar2.at[ph, pl.ds(0, R - 1)], ar_recv.at[ph, 1])
-            arout[ph, mine16] = sum(ar2[ph, i] for i in range(R))
+            wait_for(ar2.at[ph, pl.ds(0, 3)], ar_recv.at[ph, 1])
+            ar3[ph, z] = sum(ar2[ph, i] for i in range(4))
+            for peer in z_peers:
+                remote(ar3.at[ph, z], ar3.at[ph, z], ar_send.at[ph, 2], ar_recv.at[ph, 2], peer).start()
+        elif step == 3:
+            wait_for(ar3.at[ph, pl.ds(0, 3)], ar_recv.at[ph, 2])
+            arout[ph, mine16] = sum(ar3[ph, i] for i in range(4))
             for peer in line_peers:
-                remote(arout.at[ph, mine16], arout.at[ph, mine16], ar_send.at[ph, 2], ar_recv.at[ph, 2], peer).start()
+                remote(arout.at[ph, mine16], arout.at[ph, mine16], ar_send.at[ph, 3], ar_recv.at[ph, 3], peer).start()
         else:
-            wait_for(arout.at[ph, pl.ds(0, 16 * (C - 1))], ar_recv.at[ph, 2])
+            wait_for(arout.at[ph, pl.ds(0, 16 * (C - 1))], ar_recv.at[ph, 3])
 
     def reduce_finish(ph):
-        wait_for(ar1.at[ph, pl.ds(0, C - 1)], ar_send.at[ph, 0])
-        wait_for(ar2.at[ph, pl.ds(0, R - 1)], ar_send.at[ph, 1])
-        wait_for(ar1.at[ph, pl.ds(0, C - 1)], ar_send.at[ph, 2])
+        for step, count in enumerate((C - 1, 3, 3, C - 1)):
+            wait_for(ar1.at[ph, pl.ds(0, count)], ar_send.at[ph, step])
 
     am_root = col == col_to
     other_root = other == col_to
@@ -306,10 +312,13 @@
             part[0] = dot6(rows[0, col], rows[0, col], TN)
         if tick == 4:
             reduce_step(0, 0)
-        split_h(tick)
 
     gather(0, first_extra)
-    reduce_step(0, 1)
+    for i in range(n_h):
+        split_h(i)
+        if i == 3:
+            reduce_step(0, 1)
+    reduce_step(0, 2)
     gather_wait(0)
 
     def block_rows(ph, s, b):
@@ -354,7 +363,7 @@
         line_step(0, kk)
     part[1] = dot6(v_rows[...], acc[...], TN)
     reduce_step(1, 0)
-    reduce_step(0, 2)
+    reduce_step(0, 3)
     p_piece = ring_out[3]
     for j in range(3):
         wait_for(ring_in.at[j], ring_recv.at[j])
@@ -385,14 +394,17 @@
     def second_extra(tick):
         if tick == 0:
             reduce_step(1, 1)
-            reduce_step(0, 3)
-        inverse_step(tick)
+        if tick == 5:
+            reduce_step(1, 2)
 
     gather(1, second_extra)
-    reduce_step(1, 2)
+    reduce_step(1, 3)
+    reduce_step(0, 4)
+    for i in range(8):
+        inverse_step(i)
     for kk in ORDER[1:]:
         line_step(1, kk)
-    reduce_step(1, 3)
+    reduce_step(1, 4)
 
     u = inverse[...]
     middle = dot6(dot6(u, arout[1], TN), u)
@@ -429,6 +441,7 @@
     width = tiles.shape[2]
     slots = tiles.shape[0]
     steps = h_ref.shape[1] // width
+    height = 288
 
     def copy(b):
         slot = lax.rem(b, slots)
@@ -442,9 +455,12 @@
             copy(b - slots).wait()
 
         at = pl.ds(pl.multiple_of(b * width, width), width)
-        high = zhi[at]
-        change = dot1(whi[...], high, NT) + dot1(wlo[...], high, NT) + dot1(whi[...], zlo[at], NT)
-        tiles[lax.rem(b, slots)] = h_ref[:, at] - change
+        high, low = zhi[at], zlo[at]
+        for start in range(0, h_ref.shape[0], height):
+            take = pl.ds(start, height)
+            w = whi[take]
+            change = dot1(w, high, NT) + dot1(wlo[take], high, NT) + dot1(w, low, NT)
+            tiles[lax.rem(b, slots), take] = h_ref[take, at] - change
         copy(b).start()
         return carry
 
@@ -483,7 +499,8 @@
             pltpu.VMEM((piece, B), F32),
             pltpu.VMEM((2, B, B), F32),
             pltpu.VMEM((2, C, 16, B), F32),
-            pltpu.VMEM((2, R, 16, B), F32),
+            pltpu.VMEM((2, 4, 16, B), F32),
+            pltpu.VMEM((2, 4, 16, B), F32),
             pltpu.VMEM((2, B, B), F32),
             pltpu.VMEM((B, B), F32),
             pltpu.VMEM((B, B), F32),
@@ -498,8 +515,8 @@
             dma((4,)),
             dma((3,)),
             dma((3,)),
-            dma((2, 3)),
-            dma((2, 3)),
+            dma((2, 4)),
+            dma((2, 4)),
         ],
         compiler_params=pltpu.CompilerParams(
             collective_id=0, has_side_effects=True, vmem_limit_bytes=40 * 2**20
@@ -512,7 +529,7 @@
         out_shape=jax.ShapeDtypeStruct((m, n), F32),
         in_specs=[vmem] * 5,
         out_specs=hbm,
-        scratch_shapes=[pltpu.VMEM((3, m, 2 * B), F32), dma((3,))],
+        scratch_shapes=[pltpu.VMEM((2, m, 6 * B), F32), dma((2,))],
         compiler_params=pltpu.CompilerParams(vmem_limit_bytes=24 * 2**20),
         cost_estimate=pl.CostEstimate(flops=12 * m * n * B, bytes_accessed=4 * m * n, transcendentals=0),
         name="rank_update",

time: 66.3 us -> 69.4 us (1.047)
  Pallas kernels: 65.1 us -> 68.2 us
    pallas_call x1, Pallas kernels: 57.9 us -> 61.4 us  [body(): pl.pallas_call(panel_kernel, out_shape=[jax.ShapeDtypeStruct((m, n), F32)...]
where the time goes in v5:
time: 69.4 us; the launch traced here: 69.2 us
  Pallas kernels  68.2 us (98%)
  local copies, waits for them, and re-layouts  0.88 us (1%)
    pallas_call x1, Pallas kernels, body(): pl.pallas_call(panel_kernel, out_shape=[jax.ShapeDtypeStruct((m, n), F32)...  61.4 us
    pallas_call x1, Pallas kernels, body(): pl.pallas_call(update_kernel, out_shape=jax.ShapeDtypeStruct((m, n), F32)...  6.75 us

profile of v5, /device:TPU:1, one launch (start us, length us, event | category | flops | bytes accessed | tf_op | source)
XLA Modules:
  0.0 69.2 jit_solution(17032237407415269940)
XLA Ops:
  0.0 0.0 copy-start
  0.0 0.9 %copy-done = f32[144,128]{1,0:T(8,128)S(1)} copy-done((f32[144,128]{1,0:T(8,128)S(1)}, f32[144,128]{1,0:T(8,128)}, u32[]{:S(2)}) %copy-start) | copy-done | bytes 73752
  0.9 61.4 %panel_products.1 = (f32[1152,2304]{1,0:T(8,128)S(1)}, bf16[1152,256]{1,0:T(8,128)(2,1)S(1)}, bf16[1152,256]{1,0:T(8,128)(2,1)S(1)}, bf16[2304,256]{1,0:T(8,128)(2,1)S(1)}, bf16[2304,256]{1,0:T(8,128)(2,1)S(1)}) custom-call(f32[1152,2304]{1,0:T(8,128)} %h_ref.1, f32[144,128]{1,0:T(8,128)S(1)} %copy-done), custom_call_target="tpu_custom_call" | custom-call | flops 2717908992 | bytes 10616832 | tf_op jit(solution)/shard_map/panel_products/pallas_call | solution.py:478
  62.3 6.8 %rank_update.1 = f32[1152,2304]{1,0:T(8,128)} custom-call(f32[1152,2304]{1,0:T(8,128)S(1)} %get-tuple-element.10.h_ref, bf16[1152,256]{1,0:T(8,128)(2,1)S(1)} %get-tuple-element.11.whi, bf16[1152,256]{1,0:T(8,128)(2,1)S(1)} %get-tuple-element.12.wlo, bf16[2304,256]{1,0:T(8,128)(2,1)S(1)} %get-tuple-element.13.zhi, bf16[2304,256]{1,0:T(8,128)(2,1)S(1)} %get-tuple-element.14.zlo), custom_call_target="tpu_custom_call" | custom-call | flops 4076863488 | bytes 10616832 | tf_op jit(solution)/shard_map/rank_update/pallas_call | solution.py:527
Async XLA Ops:
  0.0 0.9 %copy-start = (f32[144,128]{1,0:T(8,128)S(1)}, f32[144,128]{1,0:T(8,128)}, u32[]{:S(2)}) copy-start(f32[144,128]{1,0:T(8,128)} %panel_ref.1) | copy-start | bytes 221188

commit v6 on v4

--- a/solution.py
+++ b/solution.py
@@ -385,11 +385,12 @@
     def second_extra(tick):
         if tick == 0:
             reduce_step(1, 1)
-            reduce_step(0, 3)
-        inverse_step(tick)
 
     gather(1, second_extra)
     reduce_step(1, 2)
+    reduce_step(0, 3)
+    for i in range(8):
+        inverse_step(i)
     for kk in ORDER[1:]:
         line_step(1, kk)
     reduce_step(1, 3)
@@ -429,6 +430,7 @@
     width = tiles.shape[2]
     slots = tiles.shape[0]
     steps = h_ref.shape[1] // width
+    height = 288
 
     def copy(b):
         slot = lax.rem(b, slots)
@@ -442,9 +444,12 @@
             copy(b - slots).wait()
 
         at = pl.ds(pl.multiple_of(b * width, width), width)
-        high = zhi[at]
-        change = dot1(whi[...], high, NT) + dot1(wlo[...], high, NT) + dot1(whi[...], zlo[at], NT)
-        tiles[lax.rem(b, slots)] = h_ref[:, at] - change
+        high, low = zhi[at], zlo[at]
+        for start in range(0, h_ref.shape[0], height):
+            take = pl.ds(start, height)
+            w = whi[take]
+            change = dot1(w, high, NT) + dot1(wlo[take], high, NT) + dot1(w, low, NT)
+            tiles[lax.rem(b, slots), take] = h_ref[take, at] - change
         copy(b).start()
         return carry
 
@@ -506,13 +511,13 @@
         ),
         cost_estimate=pl.CostEstimate(flops=8 * m * n * B, bytes_accessed=4 * m * n, transcendentals=0),
         name="panel_products",
-    )(hamiltonian, panel)
+    )(hamiltonian, pltpu.with_memory_space_constraint(panel, pltpu.HBM))
     return pl.pallas_call(
         update_kernel,
         out_shape=jax.ShapeDtypeStruct((m, n), F32),
         in_specs=[vmem] * 5,
         out_specs=hbm,
-        scratch_shapes=[pltpu.VMEM((3, m, 2 * B), F32), dma((3,))],
+        scratch_shapes=[pltpu.VMEM((2, m, 6 * B), F32), dma((2,))],
         compiler_params=pltpu.CompilerParams(vmem_limit_bytes=24 * 2**20),
         cost_estimate=pl.CostEstimate(flops=12 * m * n * B, bytes_accessed=4 * m * n, transcendentals=0),
         name="rank_update",

time: 66.3 us -> 64.5 us (0.973)
  Pallas kernels: 65.1 us -> 64.2 us
  local copies, waits for them, and re-layouts: 0.88 us -> 0 us
    unnamed x2 -> x0, local copies, waits for them, and re-layouts: 0.88 us -> none
where the time goes in v6:
time: 64.5 us; the launch traced here: 64.4 us
  Pallas kernels  64.2 us (100%)
    pallas_call x1, Pallas kernels, body(): pl.pallas_call(panel_kernel, out_shape=[jax.ShapeDtypeStruct((m, n), F32)...  57.5 us
    pallas_call x1, Pallas kernels, body(): pl.pallas_call(update_kernel, out_shape=jax.ShapeDtypeStruct((m, n), F32)...  6.74 us

profile of v6, /device:TPU:1, one launch (start us, length us, event | category | flops | bytes accessed | tf_op | source)
XLA Modules:
  0.0 64.4 jit_solution(2940452635293825141)
XLA Ops:
  0.0 57.5 %panel_products.1 = (f32[1152,2304]{1,0:T(8,128)S(1)}, bf16[1152,256]{1,0:T(8,128)(2,1)S(1)}, bf16[1152,256]{1,0:T(8,128)(2,1)S(1)}, bf16[2304,256]{1,0:T(8,128)(2,1)S(1)}, bf16[2304,256]{1,0:T(8,128)(2,1)S(1)}) custom-call(f32[1152,2304]{1,0:T(8,128)} %h_ref.1, f32[144,128]{1,0:T(8,128)} %panel_ref.1), custom_call_target="tpu_custom_call" | custom-call | flops 2717908992 | bytes 10616832 | tf_op jit(solution)/shard_map/panel_products/pallas_call | solution.py:467
  57.5 6.7 %rank_update.1 = f32[1152,2304]{1,0:T(8,128)} custom-call(f32[1152,2304]{1,0:T(8,128)S(1)} %get-tuple-element.10.h_ref, bf16[1152,256]{1,0:T(8,128)(2,1)S(1)} %get-tuple-element.11.whi, bf16[1152,256]{1,0:T(8,128)(2,1)S(1)} %get-tuple-element.12.wlo, bf16[2304,256]{1,0:T(8,128)(2,1)S(1)} %get-tuple-element.13.zhi, bf16[2304,256]{1,0:T(8,128)(2,1)S(1)} %get-tuple-element.14.zlo), custom_call_target="tpu_custom_call" | custom-call | flops 4076863488 | bytes 10616832 | tf_op jit(solution)/shard_map/rank_update/pallas_call | solution.py:515

commit v7 on v6

--- a/solution.py
+++ b/solution.py
@@ -322,8 +322,6 @@
             hi, lo = halves(block_rows(0, s, b))
             vw[at, :B] = hi
             vw[at, B:] = lo
-            zhi[at, :B] = hi
-            zlo[at, :B] = lo
 
     order = (2, 1, -1, 0)
     two_rows = 2 * piece
@@ -409,6 +407,8 @@
         whi[at, B:] = hi
         wlo[at, B:] = lo
 
+    zhi[:, :B] = vw[:, :B]
+    zlo[:, :B] = vw[:, B:]
     gather_wait(1)
     for b in range(blocks):
         for s in range(2):

time: 64.5 us -> 64.7 us (level)
  no operation moved by 1% of the time
where the time goes in v7:
time: 64.7 us; the launch traced here: 64.6 us
  Pallas kernels  64.4 us (100%)
    pallas_call x1, Pallas kernels, body(): pl.pallas_call(panel_kernel, out_shape=[jax.ShapeDtypeStruct((m, n), F32)...  57.7 us
    pallas_call x1, Pallas kernels, body(): pl.pallas_call(update_kernel, out_shape=jax.ShapeDtypeStruct((m, n), F32)...  6.75 us

profile of v7, /device:TPU:1, one launch (start us, length us, event | category | flops | bytes accessed | tf_op | source)
XLA Modules:
  0.0 64.6 jit_solution(6441570432055461304)
XLA Ops:
  0.0 57.7 %panel_products.1 = (f32[1152,2304]{1,0:T(8,128)S(1)}, bf16[1152,256]{1,0:T(8,128)(2,1)S(1)}, bf16[1152,256]{1,0:T(8,128)(2,1)S(1)}, bf16[2304,256]{1,0:T(8,128)(2,1)S(1)}, bf16[2304,256]{1,0:T(8,128)(2,1)S(1)}) custom-call(f32[1152,2304]{1,0:T(8,128)} %h_ref.1, f32[144,128]{1,0:T(8,128)} %panel_ref.1), custom_call_target="tpu_custom_call" | custom-call | flops 2717908992 | bytes 10616832 | tf_op jit(solution)/shard_map/panel_products/pallas_call | solution.py:467
  57.7 6.8 %rank_update.1 = f32[1152,2304]{1,0:T(8,128)} custom-call(f32[1152,2304]{1,0:T(8,128)S(1)} %get-tuple-element.10.h_ref, bf16[1152,256]{1,0:T(8,128)(2,1)S(1)} %get-tuple-element.11.whi, bf16[1152,256]{1,0:T(8,128)(2,1)S(1)} %get-tuple-element.12.wlo, bf16[2304,256]{1,0:T(8,128)(2,1)S(1)} %get-tuple-element.13.zhi, bf16[2304,256]{1,0:T(8,128)(2,1)S(1)} %get-tuple-element.14.zlo), custom_call_target="tpu_custom_call" | custom-call | flops 4076863488 | bytes 10616832 | tf_op jit(solution)/shard_map/rank_update/pallas_call | solution.py:515
